TPU v7x, 32 devices: a whole 2x2x4 slice. The times are simulated.
32 devices in a mesh: dp: 2 (over x), hd: 4 (over z), sq: 4 (over y, core).
Axes of the slice: x: 2, y: 2, z: 4, core: 2. Of those that a mesh axis runs over, the one named last changes fastest.
Arguments:
- inputs: bfloat16 [4, 1024, 2048], P('dp', ('hd', 'sq')), may hold values from -6 to 6
- cotangent: bfloat16 [4, 1024, 2048], P('dp', ('hd', 'sq')), may hold values from -6 to 6
- w_query: bfloat16 [2048, 2048], P(('dp', 'hd', 'sq')), may hold values from -0.25 to 0.25
- w_key: bfloat16 [2048, 2048], P(('dp', 'hd', 'sq')), may hold values from -0.125 to 0.125
- w_value: bfloat16 [2048, 2048], P(('dp', 'hd', 'sq')), may hold values from -0.125 to 0.125
- w_out: bfloat16 [2048, 2048], P(('dp', 'hd', 'sq')), may hold values from -0.5 to 0.5
- b_query: bfloat16 [2048], P(('dp', 'hd', 'sq')), may hold values from -3 to 3
- b_value: bfloat16 [2048], P(('dp', 'hd', 'sq')), may hold values from -0.59765625 to 0.59765625
- b_out: bfloat16 [2048], P(('dp', 'hd', 'sq')), may hold values from -1.796875 to 1.796875
- ln1_gain: bfloat16 [2048], P(('dp', 'hd', 'sq')), may hold values from 0.099609375 to 1.8984375
- ln1_bias: bfloat16 [2048], P(('dp', 'hd', 'sq')), may hold values from -1.796875 to 1.796875
- w_up: bfloat16 [2048, 8192], P(('dp', 'hd', 'sq')), may hold values from -0.125 to 0.125
- b_up: bfloat16 [8192], P(('dp', 'hd', 'sq')), may hold values from -3 to 3
- w_down: bfloat16 [8192, 2048], P(('dp', 'hd', 'sq')), may hold values from -0.0625 to 0.0625
- b_down: bfloat16 [2048], P(('dp', 'hd', 'sq')), may hold values from -1.796875 to 1.796875
- ln2_gain: bfloat16 [2048], P(('dp', 'hd', 'sq')), may hold values from 0.099609375 to 1.8984375
- ln2_bias: bfloat16 [2048], P(('dp', 'hd', 'sq')), may hold values from -1.796875 to 1.796875
Outputs:
- outputs: bfloat16 [4, 1024, 2048], P('dp', ('hd', 'sq'))
- input_grad: float32 [4, 1024, 2048], P('dp', ('hd', 'sq'))
- grad_w_query: float32 [2048, 2048], P(('dp', 'hd', 'sq'))
- grad_w_key: float32 [2048, 2048], P(('dp', 'hd', 'sq'))
- grad_w_value: float32 [2048, 2048], P(('dp', 'hd', 'sq'))
- grad_w_out: float32 [2048, 2048], P(('dp', 'hd', 'sq'))
- grad_b_query: float32 [2048], P(('dp', 'hd', 'sq'))
- grad_b_value: float32 [2048], P(('dp', 'hd', 'sq'))
- grad_b_out: float32 [2048], P(('dp', 'hd', 'sq'))
- grad_ln1_gain: float32 [2048], P(('dp', 'hd', 'sq'))
- grad_ln1_bias: float32 [2048], P(('dp', 'hd', 'sq'))
- grad_w_up: float32 [2048, 8192], P(('dp', 'hd', 'sq'))
- grad_b_up: float32 [8192], P(('dp', 'hd', 'sq'))
- grad_w_down: float32 [8192, 2048], P(('dp', 'hd', 'sq'))
- grad_b_down: float32 [2048], P(('dp', 'hd', 'sq'))
- grad_ln2_gain: float32 [2048], P(('dp', 'hd', 'sq'))
- grad_ln2_bias: float32 [2048], P(('dp', 'hd', 'sq'))
All inputs are finite; a program needn't handle non-finite values.
Results may differ from a plain program's by a relative error of at most 0.025.
Values may be sent and summed in bfloat16 or wider, within the bound.
A program may use at most 288 MiB of HBM per device.

v0:
```python
import jax
import jax.numpy as jnp
from jax import lax
from jax.sharding import PartitionSpec as P

HD = 128


EPSILON = 1e-12
NEG_FLOOR = -1e30


def layer_norm(values, gamma_vec, beta_vec):
    average = jnp.mean(values, axis=-1, keepdims=True)
    centred = values - average
    variance = jnp.mean(centred * centred, axis=-1, keepdims=True)
    return centred * lax.rsqrt(variance + EPSILON) * gamma_vec + beta_vec


def matmul(left_side, right_side):
    return jnp.dot(left_side, right_side, preferred_element_type=jnp.float32)


def matmul_left(left_side, right_side):
    return lax.dot_general(
        left_side, right_side, (((0,), (0,)), ((), ())), preferred_element_type=jnp.float32
    )


def matmul_right(left_side, right_side):
    return lax.dot_general(
        left_side, right_side, (((1,), (1,)), ((), ())), preferred_element_type=jnp.float32
    )


def smooth_gate(values):
    return jax.nn.gelu(values, approximate=True)


def column_sum(values):
    return jnp.sum(values, axis=0, dtype=jnp.float32)


def as_float(values):
    return values.astype(jnp.float32)


def fetch_attention(shards):
    w_query, w_key, w_value, w_out, b_query, b_value, b_out, gamma_one, beta_one = shards
    return (
        lax.all_gather(w_query, ("dp", "hd", "sq"), axis=0, tiled=True),
        lax.all_gather(w_key, ("dp", "hd", "sq"), axis=0, tiled=True),
        lax.all_gather(w_value, ("dp", "hd", "sq"), axis=0, tiled=True),
        lax.all_gather(w_out, ("dp", "hd", "sq"), axis=0, tiled=True),
        lax.all_gather(b_query, ("dp", "hd", "sq"), axis=0, tiled=True),
        lax.all_gather(b_value, ("dp", "hd", "sq"), axis=0, tiled=True),
        lax.all_gather(b_out, ("dp", "hd", "sq"), axis=0, tiled=True),
        lax.all_gather(gamma_one, ("dp", "hd", "sq"), axis=0, tiled=True),
        lax.all_gather(beta_one, ("dp", "hd", "sq"), axis=0, tiled=True),
    )


def fetch_mlp(shards):
    w_up, b_up, w_down, b_down, gamma_two, beta_two = shards
    return (
        lax.all_gather(w_up, ("dp", "hd", "sq"), axis=0, tiled=True),
        lax.all_gather(b_up, ("dp", "hd", "sq"), axis=0, tiled=True),
        lax.all_gather(w_down, ("dp", "hd", "sq"), axis=0, tiled=True),
        lax.all_gather(b_down, ("dp", "hd", "sq"), axis=0, tiled=True),
        lax.all_gather(gamma_two, ("dp", "hd", "sq"), axis=0, tiled=True),
        lax.all_gather(beta_two, ("dp", "hd", "sq"), axis=0, tiled=True),
    )


def whole_zeros(shards):
    devices = lax.axis_size(("dp", "hd", "sq"))
    return tuple(
        (jnp.zeros((piece.shape[0] * devices,) + piece.shape[1:], jnp.float32) for piece in shards)
    )


def attention_forward(row_in, attn_full, score_scale):
    w_query, w_key, w_value, w_out, b_query, b_value, b_out, gamma_one, beta_one = attn_full
    queries = (matmul(row_in, w_query) + as_float(b_query)).astype(jnp.bfloat16)
    keys_tok = matmul(row_in, w_key).astype(jnp.bfloat16)
    values_tok = (matmul(row_in, w_value) + as_float(b_value)).astype(jnp.bfloat16)
    queries, keys_loc, values_loc = (
        lax.all_to_all(queries, "hd", split_axis=1, concat_axis=0, tiled=True),
        lax.all_to_all(keys_tok, "hd", split_axis=1, concat_axis=0, tiled=True),
        lax.all_to_all(values_tok, "hd", split_axis=1, concat_axis=0, tiled=True),
    )
    row_count = queries.shape[0]
    head_width = queries.shape[1]
    groups = head_width // HD
    query_heads = queries.reshape(row_count, groups, HD)
    row_max = jnp.full((row_count, groups), NEG_FLOOR, jnp.float32)
    key_block = lax.all_gather(keys_loc, "sq", axis=0, tiled=True).reshape(-1, groups, HD)
    value_block = lax.all_gather(values_loc, "sq", axis=0, tiled=True).reshape(-1, groups, HD)
    scores = (
        jnp.einsum("qhd,khd->qhk", query_heads, key_block, preferred_element_type=jnp.float32)
        * score_scale
    )
    new_max = jnp.maximum(row_max, jnp.max(scores, axis=-1))
    exp_scores = jnp.exp(scores - new_max[:, :, None])
    row_total = jnp.sum(exp_scores, axis=-1)
    context = jnp.einsum(
        "qhk,khd->qhd",
        exp_scores.astype(jnp.bfloat16),
        value_block,
        preferred_element_type=jnp.float32,
    )
    row_max, row_total, context = (new_max, row_total, context)
    context = context / row_total[:, :, None]
    log_total = row_max + jnp.log(row_total)
    context_rows = context.reshape(row_count, head_width)
    context_tok = lax.all_to_all(
        context_rows.astype(jnp.bfloat16), "hd", split_axis=0, concat_axis=1, tiled=True
    )
    first_in = as_float(row_in) + matmul(context_tok, w_out) + as_float(b_out)
    normed_one = layer_norm(first_in, as_float(gamma_one), as_float(beta_one))
    kept_attn = (query_heads, keys_loc, values_loc, context_rows, log_total, context_tok, first_in)
    return (normed_one, kept_attn)


def feed_forward(normed_one, mlp_full):
    w_up, b_up, w_down, b_down, gamma_two, beta_two = mlp_full
    hidden = matmul(normed_one.astype(jnp.bfloat16), w_up) + as_float(b_up)
    activated = smooth_gate(hidden).astype(jnp.bfloat16)
    second_in = normed_one + matmul(activated, w_down) + as_float(b_down)
    return (layer_norm(second_in, as_float(gamma_two), as_float(beta_two)), (hidden, second_in))


def feed_back(cot_row, normed_one, kept_mlp, mlp_full):
    w_up, b_up, w_down, b_down, gamma_two, beta_two = mlp_full
    hidden, second_in = kept_mlp
    unused, norm_back = jax.vjp(layer_norm, second_in, as_float(gamma_two), as_float(beta_two))
    grad_second, grad_gamma, grad_beta = norm_back(cot_row)
    grad_branch = grad_second.astype(jnp.bfloat16)
    activated = smooth_gate(hidden).astype(jnp.bfloat16)
    grad_act = matmul_right(grad_branch, w_down)
    unused_gate, gate_back = jax.vjp(smooth_gate, hidden)
    grad_hidden = gate_back(grad_act)[0].astype(jnp.bfloat16)
    grad_first = grad_second + matmul_right(grad_hidden, w_up)
    pieces = (
        normed_one.astype(jnp.bfloat16),
        grad_hidden,
        activated,
        grad_branch,
        grad_gamma,
        grad_beta,
    )
    return (grad_first, pieces)


def attention_back(grad_first, row_in, kept_attn, attn_full, score_scale, totals):
    w_query, w_key, w_value, w_out, b_query, b_value, b_out, gamma_one, beta_one = attn_full
    query_heads, keys_loc, values_loc, context_rows, log_total, context_tok, first_in = kept_attn
    unused, norm_back = jax.vjp(layer_norm, first_in, as_float(gamma_one), as_float(beta_one))
    grad_first_in, grad_gamma, grad_beta = norm_back(grad_first)
    grad_branch = grad_first_in.astype(jnp.bfloat16)
    grad_wout = matmul_left(context_tok, grad_branch)
    grad_context = matmul_right(grad_branch, w_out).astype(jnp.bfloat16)
    grad_context = lax.all_to_all(grad_context, "hd", split_axis=1, concat_axis=0, tiled=True)
    row_count, head_width = grad_context.shape
    groups = head_width // HD
    grad_heads = grad_context.reshape(row_count, groups, HD)
    delta = jnp.sum((as_float(grad_context) * context_rows).reshape(row_count, groups, HD), axis=-1)
    keys_all, values_all = (
        lax.all_gather(keys_loc, "sq", axis=0, tiled=True),
        lax.all_gather(values_loc, "sq", axis=0, tiled=True),
    )
    blocks = keys_all.shape[0] // row_count
    key_blocks = keys_all.reshape(blocks, row_count, groups, HD)
    value_blocks = values_all.reshape(blocks, row_count, groups, HD)

    def sweep(grad_query, pieces):
        key_block, value_block = pieces
        scores = (
            jnp.einsum("qhd,khd->qhk", query_heads, key_block, preferred_element_type=jnp.float32)
            * score_scale
        )
        softmaxed = jnp.exp(scores - log_total[:, :, None])
        grad_value = jnp.einsum(
            "qhk,qhd->khd",
            softmaxed.astype(jnp.bfloat16),
            grad_heads,
            preferred_element_type=jnp.float32,
        )
        grad_probs = jnp.einsum(
            "qhd,khd->qhk", grad_heads, value_block, preferred_element_type=jnp.float32
        )
        grad_scores = (softmaxed * (grad_probs - delta[:, :, None])).astype(jnp.bfloat16)
        grad_query = (
            grad_query
            + jnp.einsum("qhk,khd->qhd", grad_scores, key_block, preferred_element_type=jnp.float32)
            * score_scale
        )
        grad_key = (
            jnp.einsum("qhk,qhd->khd", grad_scores, query_heads, preferred_element_type=jnp.float32)
            * score_scale
        )
        stacked = jnp.concatenate(
            (grad_key.reshape(row_count, head_width), grad_value.reshape(row_count, head_width)),
            axis=1,
        )
        return (grad_query, stacked)

    grad_query, stacked_terms = lax.scan(
        sweep, jnp.zeros((row_count, groups, HD), jnp.float32), (key_blocks, value_blocks)
    )
    kv_summed = lax.psum_scatter(
        stacked_terms.reshape(blocks * row_count, 2 * head_width).astype(jnp.bfloat16),
        "sq",
        scatter_dimension=0,
        tiled=True,
    ).astype(jnp.float32)
    grad_q = grad_query.reshape(row_count, head_width).astype(jnp.bfloat16)
    grad_k = kv_summed[:, :head_width].astype(jnp.bfloat16)
    grad_v = kv_summed[:, head_width:].astype(jnp.bfloat16)
    grad_q, grad_k, grad_v = (
        lax.all_to_all(grad_q, "hd", split_axis=0, concat_axis=1, tiled=True),
        lax.all_to_all(grad_k, "hd", split_axis=0, concat_axis=1, tiled=True),
        lax.all_to_all(grad_v, "hd", split_axis=0, concat_axis=1, tiled=True),
    )
    terms = (
        matmul_left(row_in, grad_q),
        matmul_left(row_in, grad_k),
        matmul_left(row_in, grad_v),
        grad_wout,
        column_sum(grad_q),
        column_sum(grad_v),
        column_sum(grad_branch),
        grad_gamma,
        grad_beta,
    )
    grad_input = (
        grad_first_in
        + matmul_right(grad_q, w_query)
        + matmul_right(grad_k, w_key)
        + matmul_right(grad_v, w_value)
    )
    return (grad_input, jax.tree.map(jnp.add, totals, terms))


def per_device(
    inputs,
    cotangent,
    w_query,
    w_key,
    w_value,
    w_out,
    b_query,
    b_value,
    b_out,
    ln1_gain,
    ln1_bias,
    w_up,
    b_up,
    w_down,
    b_down,
    ln2_gain,
    ln2_bias,
):
    batches = inputs.shape[0]
    score_scale = HD ** (-0.5)
    attn_shards = (w_query, w_key, w_value, w_out, b_query, b_value, b_out, ln1_gain, ln1_bias)
    mlp_shards = (w_up, b_up, w_down, b_down, ln2_gain, ln2_bias)
    normed_ones = []
    kept_attns = []
    for sample in range(batches):
        attn_full = fetch_attention(attn_shards)
        normed_one, kept_attn = attention_forward(inputs[sample], attn_full, score_scale)
        normed_ones.append(normed_one)
        kept_attns.append(kept_attn)
    results = []
    kept_mlps = []
    for sample in range(batches):
        mlp_full = fetch_mlp(mlp_shards)
        result, kept_mlp = feed_forward(normed_ones[sample], mlp_full)
        results.append(result.astype(jnp.bfloat16))
        kept_mlps.append(kept_mlp)
    grad_firsts = []
    saved_pieces = []
    for sample in range(batches):
        mlp_full = fetch_mlp(mlp_shards)
        grad_first, pieces = feed_back(
            as_float(cotangent[sample]), normed_ones[sample], kept_mlps[sample], mlp_full
        )
        grad_firsts.append(grad_first)
        saved_pieces.append(pieces)
    normed_rows = jnp.concatenate([piece[0] for piece in saved_pieces], axis=0)
    hidden_grads = jnp.concatenate([piece[1] for piece in saved_pieces], axis=0)
    act_rows = jnp.concatenate([piece[2] for piece in saved_pieces], axis=0)
    branch_grads = jnp.concatenate([piece[3] for piece in saved_pieces], axis=0)
    grad_w_up = matmul_left(normed_rows, hidden_grads)
    grad_b_up = column_sum(hidden_grads)
    grad_w_down = matmul_left(act_rows, branch_grads)
    grad_b_down = column_sum(branch_grads)
    grad_ln2_gain = reduce_terms([piece[4] for piece in saved_pieces])
    grad_ln2_bias = reduce_terms([piece[5] for piece in saved_pieces])
    grad_w_up, grad_b_up, grad_w_down, grad_b_down, grad_ln2_gain, grad_ln2_bias = (
        lax.psum_scatter(grad_w_up, ("dp", "hd", "sq"), scatter_dimension=0, tiled=True),
        lax.psum_scatter(grad_b_up, ("dp", "hd", "sq"), scatter_dimension=0, tiled=True),
        lax.psum_scatter(grad_w_down, ("dp", "hd", "sq"), scatter_dimension=0, tiled=True),
        lax.psum_scatter(grad_b_down, ("dp", "hd", "sq"), scatter_dimension=0, tiled=True),
        lax.psum_scatter(grad_ln2_gain, ("dp", "hd", "sq"), scatter_dimension=0, tiled=True),
        lax.psum_scatter(grad_ln2_bias, ("dp", "hd", "sq"), scatter_dimension=0, tiled=True),
    )
    attn_totals = whole_zeros(attn_shards)
    input_rows = []
    for sample in range(batches):
        attn_full = fetch_attention(attn_shards)
        grad_input, attn_totals = attention_back(
            grad_firsts[sample],
            inputs[sample],
            kept_attns[sample],
            attn_full,
            score_scale,
            attn_totals,
        )
        input_rows.append(grad_input)
    (
        grad_w_query,
        grad_w_key,
        grad_w_value,
        grad_w_out,
        grad_b_query,
        grad_b_value,
        grad_b_out,
        grad_ln1_gain,
        grad_ln1_bias,
    ) = attn_totals
    (
        grad_w_query,
        grad_w_key,
        grad_w_value,
        grad_w_out,
        grad_b_query,
        grad_b_value,
        grad_b_out,
        grad_ln1_gain,
        grad_ln1_bias,
    ) = (
        lax.psum_scatter(grad_w_query, ("dp", "hd", "sq"), scatter_dimension=0, tiled=True),
        lax.psum_scatter(grad_w_key, ("dp", "hd", "sq"), scatter_dimension=0, tiled=True),
        lax.psum_scatter(grad_w_value, ("dp", "hd", "sq"), scatter_dimension=0, tiled=True),
        lax.psum_scatter(grad_w_out, ("dp", "hd", "sq"), scatter_dimension=0, tiled=True),
        lax.psum_scatter(grad_b_query, ("dp", "hd", "sq"), scatter_dimension=0, tiled=True),
        lax.psum_scatter(grad_b_value, ("dp", "hd", "sq"), scatter_dimension=0, tiled=True),
        lax.psum_scatter(grad_b_out, ("dp", "hd", "sq"), scatter_dimension=0, tiled=True),
        lax.psum_scatter(grad_ln1_gain, ("dp", "hd", "sq"), scatter_dimension=0, tiled=True),
        lax.psum_scatter(grad_ln1_bias, ("dp", "hd", "sq"), scatter_dimension=0, tiled=True),
    )
    outputs = jnp.stack(results, axis=0)
    input_grad = jnp.stack(input_rows, axis=0)
    return (
        outputs,
        input_grad,
        grad_w_query,
        grad_w_key,
        grad_w_value,
        grad_w_out,
        grad_b_query,
        grad_b_value,
        grad_b_out,
        grad_ln1_gain,
        grad_ln1_bias,
        grad_w_up,
        grad_b_up,
        grad_w_down,
        grad_b_down,
        grad_ln2_gain,
        grad_ln2_bias,
    )


def reduce_terms(terms):
    total = terms[0]
    for extra in terms[1:]:
        total = total + extra
    return total


def solution(mesh):
    return jax.shard_map(
        per_device,
        mesh=mesh,
        in_specs=(
            P("dp", ("hd", "sq"), None),
            P("dp", ("hd", "sq"), None),
            P(("dp", "hd", "sq"), None),
            P(("dp", "hd", "sq"), None),
            P(("dp", "hd", "sq"), None),
            P(("dp", "hd", "sq"), None),
            P(("dp", "hd", "sq")),
            P(("dp", "hd", "sq")),
            P(("dp", "hd", "sq")),
            P(("dp", "hd", "sq")),
            P(("dp", "hd", "sq")),
            P(("dp", "hd", "sq"), None),
            P(("dp", "hd", "sq")),
            P(("dp", "hd", "sq"), None),
            P(("dp", "hd", "sq")),
            P(("dp", "hd", "sq")),
            P(("dp", "hd", "sq")),
        ),
        out_specs=(
            P("dp", ("hd", "sq"), None),
            P("dp", ("hd", "sq"), None),
            P(("dp", "hd", "sq"), None),
            P(("dp", "hd", "sq"), None),
            P(("dp", "hd", "sq"), None),
            P(("dp", "hd", "sq"), None),
            P(("dp", "hd", "sq")),
            P(("dp", "hd", "sq")),
            P(("dp", "hd", "sq")),
            P(("dp", "hd", "sq")),
            P(("dp", "hd", "sq")),
            P(("dp", "hd", "sq"), None),
            P(("dp", "hd", "sq")),
            P(("dp", "hd", "sq"), None),
            P(("dp", "hd", "sq")),
            P(("dp", "hd", "sq")),
            P(("dp", "hd", "sq")),
        ),
        check_vma=False,
    )
```

profile of v0, /device:TPU:17, one launch (start us, length us, event | category | flops | bytes accessed | tf_op | source)
XLA Modules:
  0.0 3341.9 jit_solution(1742988590803523062)
XLA Ops:
  9.5 80.0 %all-gather.16.cloned.1.call-done = bf16[2048,2048]{1,0:T(8,128)(2,1)} async-done(((bf16[64,2048]{1,0:T(8,128)(2,1)}), bf16[2048,2048]{1,0:T(8,128)(2,1)}) %all-gather.16.cloned.1.call-update) | async-done | bytes 8388624 | tf_op jit(solution)/shard_map/all_gather | solution.py:52
  89.5 5.0 convolution_convert_fusion.2
  94.6 12.3 all_to_all.280
  109.0 43.4 %all-reduce.18 = (bf16[2048]{0:T(1024)(128)(2,1)S(1)}, bf16[2048]{0:T(1024)(128)(2,1)S(1)}, bf16[2048]{0:T(1024)(128)(2,1)S(1)}, bf16[2048]{0:T(1024)(128)(2,1)S...) all-reduce(bf16[2048]{0:T(1024)(128)(2,1)S(1)} %dynamic-update-slic, ...), channel_id=1, replica_groups=mesh['dp'=2,'hd'=4,'sq'=4] {'dp','hd','sq'}, use_global_device_ids=true, to_apply=%add | all-reduce | flops 16384 | bytes 65536
  152.5 19.4 all-gather.12.cloned.1.call-done
  171.9 5.0 fusion.34
  176.9 12.3 all_to_all.281
  189.2 5.0 convolution_convert_fusion.3
  194.2 14.2 all_to_all.282
  208.5 5.0 fusion.32
  213.5 11.3 all_to_all.283
  226.9 27.4 all-gather.20.cloned.1.call-done
  254.3 4.9 fusion.35
  260.0 4.5 all-to-all-start.6
  264.5 5.0 fusion.33
  270.3 5.5 all-to-all-start.2
  275.8 35.2 %all-gather = bf16[32,1,256]{2,1,0:T(2,128)(2,1)S(1)} all-gather(bf16[1,1,256]{2,1,0:T(2,128)(2,1)S(1)} %reshape.331), channel_id=1, replica_groups=mesh['dp'=2,'hd'=4,'sq'=4] {'dp','hd','sq'}, dimensions={0}, use_global_device_ids=true | all-gather | bytes 16896 | tf_op jit(solution)/shard_map/all_gather | solution.py:67
  319.5 10.9 all-to-all-start.7
  346.0 4.9 all-to-all-start.3
  351.0 4.4 all-to-all-done.3
  355.4 51.1 %all-gather.22.cloned.1.call-done = bf16[2048,2048]{1,0:T(8,128)(2,1)} async-done(((bf16[64,2048]{1,0:T(8,128)(2,1)}), bf16[2048,2048]{1,0:T(8,128)(2,1)}) %all-gather.22.cloned.1.call-update) | async-done | bytes 8388624 | tf_op jit(solution)/shard_map/all_gather | solution.py:54
  406.6 5.2 fusion.138
  414.8 187.7 %all-gather.24.cloned.1.call-done = bf16[2048,8192]{1,0:T(8,128)(2,1)} async-done(((bf16[64,8192]{1,0:T(8,128)(2,1)}), bf16[2048,8192]{1,0:T(8,128)(2,1)}) %all-gather.24.cloned.1.call-update) | async-done | bytes 33554448 | tf_op jit(solution)/shard_map/all_gather | solution.py:66
  602.5 18.7 multiply_convert_fusion
  621.2 177.0 %all-gather.26.cloned.1.call-done = bf16[8192,2048]{1,0:T(8,128)(2,1)} async-done(((bf16[256,2048]{1,0:T(8,128)(2,1)}), bf16[8192,2048]{1,0:T(8,128)(2,1)}) %all-gather.26.cloned.1.call-update) | async-done | bytes 33554448 | tf_op jit(solution)/shard_map/all_gather | solution.py:68
  798.2 14.2 fusion.140
  812.7 18.1 multiply_convert_fusion.1
  830.8 14.1 fusion.139
  848.3 15.9 fusion.49
  864.2 15.9 convolution_add_fusion.15
  880.2 15.9 fusion.42
  896.1 17.2 multiply_reduce_fusion.1
  915.2 6.3 convolution_convert_fusion.1
  922.3 4.5 all-to-all-start.8
  926.9 6.1 convolution_convert_fusion
  933.8 4.8 all-to-all-start.12
  940.6 15.9 while.26
  960.5 15.5 while.27
  977.1 4.5 all-to-all-start.9
  985.8 4.9 all-to-all-start.13
  990.7 8.1 fusion.141
  1004.0 4.5 all-to-all-start.11
  1009.3 16.1 reduce-scatter.17.cloned.1.call-done
  1027.3 4.6 all-to-all-start.15
  1036.8 13.9 convolution_add_fusion.2
  1054.1 8.1 add_bitcast_fusion.2
  1062.2 17.6 copy.185
  1079.9 12.4 all_to_all.284
  1092.2 5.2 all-to-all-start.14
  1103.6 8.1 add_bitcast_fusion.1
  1111.7 17.6 copy.187
  1132.0 8.1 add_bitcast_fusion
  1140.2 17.6 copy.189
  1159.3 23.5 fusion.54
  1184.5 24.1 fusion.62
  1210.5 6.3 convolution_add_fusion.8
  1216.8 6.3 convolution_add_fusion.5
  1223.2 6.3 convolution_add_fusion.7
  1249.9 104.4 %reduce-scatter.19.cloned.1.call-done = f32[64,2048]{1,0:T(8,128)} async-done(((f32[2048,2048]{1,0:T(8,128)}), f32[64,2048]{1,0:T(8,128)}) %reduce-scatter.19.cloned.1.call-update) | async-done | bytes 524304 | tf_op jit(solution)/shard_map/reduce_scatter | solution.py:347
  1354.3 187.7 %reduce-scatter.25.cloned.1.call-done = f32[64,2048]{1,0:T(8,128)} async-done(((f32[2048,2048]{1,0:T(8,128)}), f32[64,2048]{1,0:T(8,128)}) %reduce-scatter.25.cloned.1.call-update) | async-done | bytes 524304
  1542.0 188.5 %reduce-scatter.27.cloned.1.call-done = f32[64,2048]{1,0:T(8,128)} async-done(((f32[2048,2048]{1,0:T(8,128)}), f32[64,2048]{1,0:T(8,128)}) %reduce-scatter.27.cloned.1.call-update) | async-done | bytes 524304
  1730.5 187.4 %reduce-scatter.29.cloned.1.call-done = f32[64,2048]{1,0:T(8,128)} async-done(((f32[2048,2048]{1,0:T(8,128)}), f32[64,2048]{1,0:T(8,128)}) %reduce-scatter.29.cloned.1.call-update) | async-done | bytes 524304
  1917.9 708.1 %reduce-scatter.23.cloned.1.call-done = f32[256,2048]{1,0:T(8,128)} async-done(((f32[8192,2048]{1,0:T(8,128)}), f32[256,2048]{1,0:T(8,128)}) %reduce-scatter.23.cloned.1.call-update) | async-done | bytes 2097168 | tf_op jit(solution)/shard_map/reduce_scatter | solution.py:304
  2626.0 708.9 %reduce-scatter.21.cloned.1.call-done = f32[64,8192]{1,0:T(8,128)} async-done(((f32[2048,8192]{1,0:T(8,128)}), f32[64,8192]{1,0:T(8,128)}) %reduce-scatter.21.cloned.1.call-update) | async-done | bytes 2097168 | tf_op jit(solution)/shard_map/reduce_scatter | solution.py:302
  (407 shorter events, 133.9 us)
Async XLA Ops:
  7.2 82.3 %all-gather.16.cloned.1.call-start = ((), (), s32[]{:S(2)}) async-start(), calls=%async_computation.26 | async-start | bytes 8650752 | tf_op jit(solution)/shard_map/all_gather | solution.py:52
  7.9 163.9 %all-gather.12.cloned.1.call-start = ((), (), s32[]{:S(2)}) async-start(), calls=%async_computation.24 | async-start | bytes 8650752 | tf_op jit(solution)/shard_map/all_gather | solution.py:53
  8.7 245.6 %all-gather.20.cloned.1.call-start = ((), (), s32[]{:S(2)}) async-start(), calls=%async_computation.28 | async-start | bytes 8650752 | tf_op jit(solution)/shard_map/all_gather | solution.py:51
  9.4 97.6 %copy-start.53 = (bf16[64]{0:T(256)(128)(2,1)S(1)}, bf16[64]{0:T(256)(128)(2,1)}, u32[]{:S(2)}) copy-start(bf16[64]{0:T(256)(128)(2,1)} %param.28) | copy-start | bytes 388
  9.4 97.8 %copy-start.54 = (bf16[64]{0:T(256)(128)(2,1)S(1)}, bf16[64]{0:T(256)(128)(2,1)}, u32[]{:S(2)}) copy-start(bf16[64]{0:T(256)(128)(2,1)} %param.27) | copy-start | bytes 388
  9.4 98.1 %copy-start.55 = (bf16[64]{0:T(256)(128)(2,1)S(1)}, bf16[64]{0:T(256)(128)(2,1)}, u32[]{:S(2)}) copy-start(bf16[64]{0:T(256)(128)(2,1)} %param.29) | copy-start | bytes 388
  9.4 98.3 %copy-start.56 = (bf16[64]{0:T(256)(128)(2,1)S(1)}, bf16[64]{0:T(256)(128)(2,1)}, u32[]{:S(2)}) copy-start(bf16[64]{0:T(256)(128)(2,1)} %param.30) | copy-start | bytes 388
  9.5 98.6 %copy-start.57 = (bf16[64]{0:T(256)(128)(2,1)S(1)}, bf16[64]{0:T(256)(128)(2,1)}, u32[]{:S(2)}) copy-start(bf16[64]{0:T(256)(128)(2,1)} %param.31) | copy-start | bytes 388
  9.5 98.8 %copy-start.58 = (bf16[64]{0:T(256)(128)(2,1)S(1)}, bf16[64]{0:T(256)(128)(2,1)}, u32[]{:S(2)}) copy-start(bf16[64]{0:T(256)(128)(2,1)} %param.35) | copy-start | bytes 388
  9.5 99.1 %copy-start.59 = (bf16[64]{0:T(256)(128)(2,1)S(1)}, bf16[64]{0:T(256)(128)(2,1)}, u32[]{:S(2)}) copy-start(bf16[64]{0:T(256)(128)(2,1)} %param.36) | copy-start | bytes 388
  9.5 99.3 %copy-start.60 = (bf16[64]{0:T(256)(128)(2,1)S(1)}, bf16[64]{0:T(256)(128)(2,1)}, u32[]{:S(2)}) copy-start(bf16[64]{0:T(256)(128)(2,1)} %param.37) | copy-start | bytes 388
  9.5 162.4 %copy-start.1 = (bf16[2,64,2048]{2,1,0:T(8,128)(2,1)S(1)}, bf16[2,64,2048]{2,1,0:T(8,128)(2,1)}, u32[]{:S(2)}) copy-start(bf16[2,64,2048]{2,1,0:T(8,128)(2,1)} %param.21) | copy-start | bytes 1572868
  9.5 302.1 %all-gather.30.cloned.1.call-start = ((), (), s32[]{:S(2)}) async-start(), calls=%async_computation.33 | async-start | bytes 1310720 | tf_op jit(solution)/shard_map/all_gather | solution.py:97
  106.9 206.2 %all-gather.28.cloned.1.call-start = ((), (), s32[]{:S(2)}) async-start(), calls=%async_computation.32 | async-start | bytes 1310720 | tf_op jit(solution)/shard_map/all_gather | solution.py:98
  189.1 141.2 %all-gather.18.cloned.1.call-start = ((), (), s32[]{:S(2)}) async-start(), calls=%async_computation.27 | async-start | bytes 1310720 | tf_op jit(solution)/shard_map/all_gather | solution.py:97
  208.4 123.5 %all-gather.14.cloned.1.call-start = ((), (), s32[]{:S(2)}) async-start(), calls=%async_computation.25 | async-start | bytes 1310720 | tf_op jit(solution)/shard_map/all_gather | solution.py:98
  224.8 181.8 %all-gather.22.cloned.1.call-start = ((), (), s32[]{:S(2)}) async-start(), calls=%async_computation.29 | async-start | bytes 8650752 | tf_op jit(solution)/shard_map/all_gather | solution.py:54
  225.5 377.0 %all-gather.24.cloned.1.call-start = ((), (), s32[]{:S(2)}) async-start(), calls=%async_computation.30 | async-start | bytes 34603008 | tf_op jit(solution)/shard_map/all_gather | solution.py:66
  226.3 572.0 %all-gather.26.cloned.1.call-start = ((), (), s32[]{:S(2)}) async-start(), calls=%async_computation.31 | async-start | bytes 34603008 | tf_op jit(solution)/shard_map/all_gather | solution.py:68
  260.0 10.3 all-to-all-start.6
  264.5 11.3 copy-start.61
  270.3 41.0 %all-to-all-start.2 = ((bf16[64,4,512]{2,0,1:T(8,128)(2,1)}), bf16[64,4,512]{2,0,1:T(8,128)(2,1)S(1)}, u32[]{:S(2)}, u32[]{:S(2)}) async-start(bf16[64,4,512]{2,0,1:T(8,128)(2,1)} %bitcast.345), calls=%async_computation.2 | async-start | bytes 524288 | tf_op jit(solution)/shard_map/all_to_all | solution.py:88
  319.5 26.5 all-to-all-start.7
  337.3 7.6 copy-start.27
  346.0 9.4 all-to-all-start.3
  351.0 60.8 %copy-start.14 = (bf16[4,8,8,512]{3,2,0,1:T(8,128)(2,1)}, bf16[4,8,8,512]{3,2,0,1:T(8,128)(2,1)S(1)}, u32[]{:S(2)}) copy-start(bf16[4,8,8,512]{3,2,0,1:T(8,128)(2,1)S(1)} %copy.244) | copy-start | bytes 786436
  355.4 56.4 %copy-start.30 = (bf16[4,8,8,512]{3,2,0,1:T(8,128)(2,1)}, bf16[4,8,8,512]{3,2,0,1:T(8,128)(2,1)S(1)}, u32[]{:S(2)}) copy-start(bf16[4,8,8,512]{3,2,0,1:T(8,128)(2,1)S(1)} %copy.243) | copy-start | bytes 786436
  414.8 206.4 %copy-start.34 = (bf16[64,2048]{1,0:T(8,128)(2,1)}, bf16[64,2048]{1,0:T(8,128)(2,1)S(1)}, u32[]{:S(2)}) copy-start(bf16[64,2048]{1,0:T(8,128)(2,1)S(1)} %get-tuple-element.375) | copy-start | bytes 786436
  414.8 397.9 %copy-start.32 = (bf16[64,2048]{1,0:T(8,128)(2,1)}, bf16[64,2048]{1,0:T(8,128)(2,1)S(1)}, u32[]{:S(2)}) copy-start(bf16[64,2048]{1,0:T(8,128)(2,1)S(1)} %get-tuple-element.374) | copy-start | bytes 786436
  830.8 14.1 copy-start.11
  830.8 14.4 copy-start.25
  847.6 32.6 copy-start.16
  848.3 15.9 copy-start.18
  864.2 16.0 copy-start.4
  896.1 17.2 copy-start.7
  915.0 11.8 copy-start.21
  922.3 11.6 all-to-all-start.8
  926.9 12.0 copy-start.48
  933.8 22.6 all-to-all-start.12
  938.6 63.5 %reduce-scatter.15.cloned.1.call-start = ((), (), s32[]{:S(2)}) async-start(), calls=%async_computation.34 | async-start | bytes 2621440 | tf_op jit(solution)/shard_map/reduce_scatter | solution.py:211
  957.8 67.7 %reduce-scatter.17.cloned.1.call-start = ((), (), s32[]{:S(2)}) async-start(), calls=%async_computation.35 | async-start | bytes 2621440 | tf_op jit(solution)/shard_map/reduce_scatter | solution.py:211
  976.0 14.6 copy-start.31
  976.1 14.6 copy-start.43
  977.1 8.7 all-to-all-start.9
  985.8 18.2 all-to-all-start.13
  990.7 10.5 copy-start.5
  990.7 10.5 copy-start.8
  990.7 17.9 copy-start.17
  990.7 17.8 copy-start.19
  998.8 38.0 %copy-start.15 = (bf16[4,8,8,512]{3,2,0,1:T(8,128)(2,1)S(1)}, bf16[4,8,8,512]{3,2,0,1:T(8,128)(2,1)}, u32[]{:S(2)}) copy-start(bf16[4,8,8,512]{3,2,0,1:T(8,128)(2,1)} %copy-done.14) | copy-start | bytes 786436
  998.8 38.0 %copy-start.41 = (bf16[64,2048]{1,0:T(8,128)(2,1)S(1)}, bf16[64,2048]{1,0:T(8,128)(2,1)}, u32[]{:S(2)}) copy-start(bf16[64,2048]{1,0:T(8,128)(2,1)} %copy-done.40) | copy-start | bytes 786436
  1004.0 23.3 all-to-all-start.11
  1027.3 8.8 all-to-all-start.15
  1031.9 206.7 %all-reduce.21.cloned.1.call-start = ((), (), s32[]{:S(2)}) async-start(), calls=%async_computation.42 | async-start | bytes 196608
  1036.8 317.5 %reduce-scatter.19.cloned.1.call-start = ((), (), s32[]{:S(2)}) async-start(), calls=%async_computation.36 | async-start | bytes 17301504 | tf_op jit(solution)/shard_map/reduce_scatter | solution.py:347
  1050.7 491.3 %reduce-scatter.25.cloned.1.call-start = ((), (), s32[]{:S(2)}) async-start(), calls=%async_computation.39 | async-start | bytes 17301504
  1092.2 9.0 all-to-all-start.14
  1097.5 633.0 %reduce-scatter.27.cloned.1.call-start = ((), (), s32[]{:S(2)}) async-start(), calls=%async_computation.40 | async-start | bytes 17301504
  1129.4 788.5 %reduce-scatter.29.cloned.1.call-start = ((), (), s32[]{:S(2)}) async-start(), calls=%async_computation.41 | async-start | bytes 17301504
  1157.8 1468.2 %reduce-scatter.23.cloned.1.call-start = ((), (), s32[]{:S(2)}) async-start(), calls=%async_computation.38 | async-start | bytes 69206016 | tf_op jit(solution)/shard_map/reduce_scatter | solution.py:304
  1182.9 2152.1 %reduce-scatter.21.cloned.1.call-start = ((), (), s32[]{:S(2)}) async-start(), calls=%async_computation.37 | async-start | bytes 69206016 | tf_op jit(solution)/shard_map/reduce_scatter | solution.py:302
  1210.5 18.9 slice-start
  1216.8 12.6 slice-start.1
  1223.1 9.0 slice-start.2
  (32 other events, 112.0 us)
Sparse Core Ops, SparseCore 0:
  10.9 78.5 all-gather.15
  92.4 79.4 all-gather.11
  174.8 79.5 all-gather.19
  255.7 15.9 all-gather.29
  273.1 16.8 all-gather.27
  291.4 16.7 all-gather.17
  309.8 16.7 all-gather.13
  329.4 77.1 all-gather.21
  409.5 192.9 all-gather.23
  605.2 192.9 all-gather.25
  957.9 32.9 reduce-scatter.14
  994.0 31.3 reduce-scatter.16
  1039.1 127.1 all-reduce.20
  1169.1 185.1 reduce-scatter.18
  1357.1 184.8 reduce-scatter.24
  1544.8 185.6 reduce-scatter.26
  1733.3 184.5 reduce-scatter.28
  1920.8 705.1 reduce-scatter.22
  2629.0 705.8 reduce-scatter.20
where the time goes:
time: 3360 us; the launch traced here: 3340 us
  waiting for transfers between devices  2660 us (79%)
  matrix products  324 us (10%)
  blocking collectives  141 us (4%)
  local copies, waits for them, and re-layouts  123 us (4%)
  starting transfers between devices  59.9 us (2%)
    reduce_scatter x1, waiting for transfers between devices, per_device(): lax.psum_scatter(grad_w_up, ('dp', 'hd', 'sq'), scatter_dimension=0, tile...  709 us
    reduce_scatter x1, waiting for transfers between devices, per_device(): lax.psum_scatter(grad_w_down, ('dp', 'hd', 'sq'), scatter_dimension=0, ti...  708 us
    unnamed x23, waiting for transfers between devices  568 us
    all_gather x1, waiting for transfers between devices, fetch_mlp(): lax.all_gather(w_up, ('dp', 'hd', 'sq'), axis=0, tiled=True)  188 us
    all_gather x1, waiting for transfers between devices, fetch_mlp(): lax.all_gather(w_down, ('dp', 'hd', 'sq'), axis=0, tiled=True)  177 us
    reduce_scatter x1, waiting for transfers between devices, per_device(): lax.psum_scatter(grad_w_out, ('dp', 'hd', 'sq'), scatter_dimension=0, til...  104 us
    dot_general x12, matrix products, matmul_right(): lax.dot_general(left_side, right_side, (((1,), (1,)), ((), ())), preferre...  104 us
    dot_general x12, matrix products, matmul(): return jnp.dot(left_side, right_side, preferred_element_type=jnp.float32)  102 us
  transfers between devices with their start and end apart: 30, of which 17 were waited for; matrix products, arithmetic and copies ran while one was open for 10% of the time, Pallas kernels for 0%

commit v1 on v0

v1 whole, which is shorter than its diff:
```python
import functools

import jax
import jax.numpy as jnp
from jax import lax
from jax.experimental import pallas as pl
from jax.experimental.pallas import tpu as pltpu
from jax.sharding import Mesh
from jax.sharding import PartitionSpec as P

F32 = jnp.float32
BF16 = jnp.bfloat16
HD = 128
EPSILON = 1e-12
TP = 8
STRIP = 16
VMEM_LIMIT = 60 * 2**20
AXES = ("x", "zh", "zl", "y", "c")
SCALE = HD ** (-0.5)


class Sizes:
    def __init__(self, groups_x, width, hidden, tokens):
        self.nx = groups_x
        self.parts = 2 * groups_x
        self.width = width
        self.hidden = hidden
        self.tokens = tokens
        self.half = tokens // 2
        self.rows_all = TP * tokens
        self.row_shard = width // (TP * self.parts)
        self.hid_shard = hidden // (TP * self.parts)
        self.pieces = HD // self.row_shard
        self.heads = width // HD // TP
        self.cols = self.heads * HD
        self.hid = hidden // TP
        self.slab = width // self.parts


class Place:
    def __init__(self, sizes):
        self.x, self.zh, self.zl, self.y, self.c = (lax.axis_index(a) for a in AXES)
        self.nx = sizes.nx
        self.t = self.zl * 4 + self.y * 2 + self.c
        self.p = self.x * 2 + self.zh
        self.pz = self.x * 2 + (1 - self.zh)
        self.to_c = {"c": 1 - self.c}
        self.to_y = {"y": 1 - self.y}
        self.to_z = {"zl": 1 - self.zl}
        self.to_h = {"zh": 1 - self.zh}

    def peer(self, flip):
        target = {}
        if flip & 4:
            target["zl"] = 1 - self.zl
        if flip & 2:
            target["y"] = 1 - self.y
        if flip & 1:
            target["c"] = 1 - self.c
        return target

    def index_of(self, flip):
        zl = 1 - self.zl if flip & 4 else self.zl
        y = 1 - self.y if flip & 2 else self.y
        c = 1 - self.c if flip & 1 else self.c
        return zl * 4 + y * 2 + c

    def to_x(self, step):
        return {"x": lax.rem(self.x + step, self.nx)}

    def x_of(self, step):
        return lax.rem(self.x + step, self.nx)


class Copies:
    def __init__(self, send, recv, local):
        self.send, self.recv, self.local_sems = send, recv, local
        self.n_remote = 0
        self.n_local = 0
        self.sent = []
        self.kept = []

    def remote(self, src, dst, target):
        i = self.n_remote
        self.n_remote += 1
        copy = pltpu.make_async_remote_copy(
            src_ref=src,
            dst_ref=dst,
            send_sem=self.send.at[i],
            recv_sem=self.recv.at[i],
            device_id=target,
            device_id_type=pl.DeviceIdType.MESH,
        )
        copy.start()
        self.sent.append(copy)
        return copy

    def local(self, src, dst):
        i = self.n_local
        self.n_local += 1
        copy = pltpu.make_async_copy(src, dst, self.local_sems.at[i])
        copy.start()
        return copy

    def keep(self, src, dst):
        self.kept.append(self.local(src, dst))

    def left(self, copy):
        copy.wait_send()
        self.sent = [other for other in self.sent if other is not copy]

    def finish(self):
        for copy in self.kept:
            copy.wait()
        for copy in self.sent:
            copy.wait_send()


def greet(targets):
    barrier = pltpu.get_barrier_semaphore()
    for target in targets:
        pl.semaphore_signal(
            barrier, inc=1, device_id=target, device_id_type=pl.DeviceIdType.MESH
        )
    pl.semaphore_wait(barrier, len(targets))


def dot(left, right):
    return jnp.dot(left, right, preferred_element_type=F32)


def dot_nt(left, right):
    return lax.dot_general(left, right, (((1,), (1,)), ((), ())), preferred_element_type=F32)


def dot_tn(left, right):
    return lax.dot_general(left, right, (((0,), (0,)), ((), ())), preferred_element_type=F32)


def tile(i, size):
    return pl.ds(pl.multiple_of(i * size, size), size)


def loop(count, body):
    def step(i, carry):
        body(i)
        return carry

    lax.fori_loop(0, count, step, 0)


def normed(values):
    average = jnp.mean(values, axis=1, keepdims=True)
    centred = values - average
    variance = jnp.mean(centred * centred, axis=1, keepdims=True)
    scale = lax.rsqrt(variance + EPSILON)
    return centred * scale, scale


def normed_back(grad, xhat, scale):
    along = jnp.mean(grad * xhat, axis=1, keepdims=True)
    return scale * (grad - jnp.mean(grad, axis=1, keepdims=True) - xhat * along)


class Gather:
    def __init__(self, net, at, sz, buf, start, count):
        self.net, self.at, self.sz, self.buf = net, at, sz, buf
        self.start, self.count = start, count
        half = sz.width // 2
        self.cols = (pl.ds(0, half), pl.ds(half, half))
        self.sib = [None] * 4

    def part(self, slot, core, cols=None):
        rows = pl.ds((slot * 2 + core) * self.sz.tokens + self.start, self.count)
        return self.buf.at[rows, :] if cols is None else self.buf.at[rows, cols]

    def send(self):
        net, at = self.net, self.at
        self.from_y = [None, None]
        self.from_z = [None, None]
        for h in (0, 1):
            self.from_y[h] = net.remote(
                self.part(0, 0, self.cols[h]), self.part(1, 0, self.cols[h]), at.to_y
            )
            self.from_z[1 - h] = net.remote(
                self.part(0, 0, self.cols[1 - h]), self.part(2, 0, self.cols[1 - h]), at.to_z
            )
        self.share(0)

    def share(self, slot):
        self.sib[slot] = self.net.remote(self.part(slot, 0), self.part(slot, 1), self.at.to_c)

    def relay(self):
        net, at = self.net, self.at
        self.from_y[0].wait_recv()
        to_z = net.remote(
            self.part(1, 0, self.cols[0]), self.part(3, 0, self.cols[0]), at.to_z
        )
        self.from_z[1].wait_recv()
        to_y = net.remote(
            self.part(2, 0, self.cols[1]), self.part(3, 0, self.cols[1]), at.to_y
        )
        self.diag = (to_z, to_y)
        self.from_y[1].wait_recv()
        self.share(1)
        self.from_z[0].wait_recv()
        self.share(2)

    def relay_last(self):
        for copy in self.diag:
            copy.wait_recv()
        self.share(3)

    def ready(self, slot):
        self.sib[slot].wait_recv()


class Scatter:
    def __init__(self, net, at, sz, bufs):
        self.net, self.at, self.sz = net, at, sz
        self.mine, self.theirs, self.got, self.diag, self.diag_got, self.out, self.inn = bufs
        self.sib = [None] * 4

    @staticmethod
    def scratch(sz):
        t, d = sz.tokens, sz.width
        return [
            pltpu.VMEM((4 * t, d), F32),
            pltpu.VMEM((4 * t, d), BF16),
            pltpu.VMEM((4 * t, d), BF16),
            pltpu.VMEM((t, d), BF16),
            pltpu.VMEM((t, d), BF16),
            pltpu.VMEM((2 * t, d), BF16),
            pltpu.VMEM((2 * t, d), BF16),
        ]

    def put(self, slot, cols, value):
        t = self.sz.tokens
        self.mine[pl.ds(slot * t, t), cols] = value[:t]
        self.theirs[pl.ds(slot * t, t), cols] = value[t:].astype(BF16)

    def share(self, slot):
        rows = pl.ds(slot * self.sz.tokens, self.sz.tokens)
        self.sib[slot] = self.net.remote(self.theirs.at[rows, :], self.got.at[rows, :], self.at.to_c)

    def add(self, slot, start, count, dst, dst_start, extra=None):
        base = slot * self.sz.tokens + start

        def body(i):
            rows = pl.ds(pl.multiple_of(base + i * STRIP, STRIP), STRIP)
            total = self.mine[rows, :] + self.got[rows, :].astype(F32)
            if extra is not None:
                there = pl.ds(pl.multiple_of(start + i * STRIP, STRIP), STRIP)
                total = total + extra[there, :].astype(F32)
            dst[pl.ds(pl.multiple_of(dst_start + i * STRIP, STRIP), STRIP), :] = total.astype(BF16)

        loop(count // STRIP, body)

    def send_diag(self):
        net, at, h = self.net, self.at, self.sz.half
        self.sib[3].wait_recv()
        self.add(3, 0, 2 * h, self.diag, 0)
        low, high = pl.ds(0, h), pl.ds(h, h)
        self.d_low = net.remote(self.diag.at[low, :], self.diag_got.at[low, :], at.to_y)
        self.d_high = net.remote(self.diag.at[high, :], self.diag_got.at[high, :], at.to_z)

    def half_out(self, side, start, target):
        rows = pl.ds(side * self.sz.tokens + start, self.sz.half)
        return self.net.remote(self.out.at[rows, :], self.inn.at[rows, :], target)

    def send_free(self):
        at, t, h = self.at, self.sz.tokens, self.sz.half
        self.sib[1].wait_recv()
        self.add(1, 0, h, self.out, 0)
        self.y_low = self.half_out(0, 0, at.to_y)
        self.sib[2].wait_recv()
        self.add(2, h, h, self.out, t + h)
        self.z_high = self.half_out(1, h, at.to_z)

    def send_joined(self):
        at, t, h = self.at, self.sz.tokens, self.sz.half
        self.d_high.wait_recv()
        self.add(1, h, h, self.out, h, self.diag_got)
        self.y_high = self.half_out(0, h, at.to_y)
        self.d_low.wait_recv()
        self.add(2, 0, h, self.out, t, self.diag_got)
        self.z_low = self.half_out(1, 0, at.to_z)

    def settle(self):
        for copy in [*self.sib, self.d_low, self.d_high, self.y_low, self.z_high, self.y_high, self.z_low]:
            self.net.left(copy)

    def wait(self):
        self.sib[0].wait_recv()
        for copy in (self.y_low, self.z_high, self.y_high, self.z_low):
            copy.wait_recv()

    def total(self, i):
        t = self.sz.tokens
        rows = tile(i, STRIP)
        far = pl.ds(pl.multiple_of(t + i * STRIP, STRIP), STRIP)
        return (
            self.mine[rows, :]
            + self.got[rows, :].astype(F32)
            + self.inn[rows, :].astype(F32)
            + self.inn[far, :].astype(F32)
        )


class Spread:
    def __init__(self, net, at, view, own, across):
        self.net, self.at, self.view = net, at, view
        self.own, self.across = own, across
        self.from_h = net.remote(view(own), view(own), at.to_h)
        self.from_x = [
            net.remote(view(own), view(own), at.to_x(step)) for step in range(1, at.nx)
        ]
        self.relayed = []

    def relay(self):
        self.from_h.wait_recv()
        self.relayed = [
            self.net.remote(self.view(self.across), self.view(self.across), self.at.to_x(step))
            for step in range(1, self.at.nx)
        ]

    def near(self):
        for copy in self.from_x:
            copy.wait_recv()

    def far(self):
        for copy in self.relayed:
            copy.wait_recv()


def attention_forward_kernel(
    sz,
    xin, wqkv_pack, wup_pack, wout, wdown, vec_pack,
    x_all, wqkv, w_out_own, w_up, w_down, vec_all, bup_all, qkv_all, ctx_all, first_in, first_all,
    xs, wq, wo_got, wo, vecs, vec, bup, acc, qkv, ctx, fin, first, *rest,
):
    *sum_bufs, send, recv, local = rest
    at = Place(sz)
    net = Copies(send, recv, local)
    t, d, h = sz.tokens, sz.width, sz.half
    rw, rf = sz.row_shard, sz.hid_shard
    flips = range(1, TP)
    greet(
        [at.peer(f) for f in flips] + [at.to_h] + [at.to_x(s) for s in range(1, sz.nx)]
    )

    own_rows = pl.ds(at.zh * h, h)
    from_h = net.remote(xin.at[1 - at.zh], xs.at[own_rows, :], at.to_h)
    own_x = net.local(xin.at[at.zh], xs.at[own_rows, :])

    def wq_rows(p, member, count=1):
        return pl.ds((p * TP + member) * rw, count * rw)

    own_wq = net.local(wqkv_pack.at[at.t], wq.at[wq_rows(at.p, at.t), :])
    own_vec = net.local(vec_pack, vecs.at[at.p * TP + at.t])
    own_wu = net.local(wup_pack.at[at.t], w_up.at[wq_rows(at.p, at.t), :])
    own_wd = net.local(wdown, w_down.at[pl.ds(at.p * rf, rf), :])
    own_wo = net.local(wout, wo_got.at[at.p])
    vec_in = [net.remote(vec_pack, vecs.at[at.p * TP + at.t], at.peer(f)) for f in flips]
    wq_in = [None] + [
        net.remote(wqkv_pack.at[at.index_of(f)], wq.at[wq_rows(at.p, at.t), :], at.peer(f))
        for f in flips
    ]
    own_x.wait()
    near_rows = Gather(net, at, sz, xs, at.zh * h, h)
    near_rows.send()

    def chip_block(buf, f):
        member = at.index_of(f) - at.c
        return lambda p: buf.at[wq_rows(p, member, 2), :]

    wq_spread = []
    for f in (0, 2, 4, 6):
        if f == 0:
            own_wq.wait()
        else:
            wq_in[f].wait_recv()
        wq_in[f + 1].wait_recv()
        wq_spread.append(Spread(net, at, chip_block(wq, f), at.p, at.pz))
    own_vec.wait()
    for copy in vec_in:
        copy.wait_recv()
    vec_spread = Spread(net, at, lambda p: vecs.at[pl.ds(p * TP, TP)], at.p, at.pz)
    wu_in = [None] + [
        net.remote(wup_pack.at[at.index_of(f)], w_up.at[wq_rows(at.p, at.t), :], at.peer(f))
        for f in flips
    ]
    from_h.wait_recv()
    far_rows = Gather(net, at, sz, xs, (1 - at.zh) * h, h)
    far_rows.send()
    near_rows.relay()
    own_wo.wait()
    wo_spread = Spread(net, at, lambda p: wo_got.at[p], at.p, at.pz)
    vec_spread.relay()
    far_rows.relay()
    near_rows.relay_last()
    far_rows.relay_last()

    def accumulate(zh, first_part):
        def body(i):
            rows = tile(i, 256)
            total = jnp.zeros((256, 3 * sz.cols), F32) if first_part else acc[rows, :]
            for x in range(sz.nx):
                block = tile(x * 2 + zh, sz.slab)
                total = total + dot(xs[rows, block], wq[block, :])
            acc[rows, :] = total

        loop(sz.rows_all // 256, body)

    for slot in range(4):
        near_rows.ready(slot)
        far_rows.ready(slot)
    for item in wq_spread:
        item.near()
    net.keep(xs, x_all)
    accumulate(at.zh, True)
    for item in wq_spread:
        item.relay()
    own_wu.wait()
    own_wd.wait()
    wu_spread = []
    for f in (0, 2, 4, 6):
        if f:
            wu_in[f].wait_recv()
        wu_in[f + 1].wait_recv()
        wu_spread.append(Spread(net, at, chip_block(w_up, f), at.p, at.pz))
    for item in wq_spread:
        item.far()
    vec_spread.near()
    vec_spread.far()
    for j in range(d // HD):
        piece = vecs[j * sz.pieces, 0:8]
        for k in range(1, sz.pieces):
            piece = piece + vecs[j * sz.pieces + k, 0:8]
        vec[:, j * HD : (j + 1) * HD] = piece
    if rf >= HD:
        for p in range(sz.parts):
            for j in range(rf // HD):
                lanes = pl.ds(p * rf + j * HD, HD)
                bup[0:1, lanes] = vecs[p * TP + at.t, 8 + j : 9 + j]
    else:
        for j in range(sz.hid // HD):
            each = HD // rf
            row = vecs[j * each * TP + at.t, 8:9]
            for k in range(1, each):
                row = row + vecs[(j * each + k) * TP + at.t, 8:9]
            bup[0:1, j * HD : (j + 1) * HD] = row
    net.keep(vec, vec_all)
    net.keep(bup, bup_all)
    accumulate(1 - at.zh, False)

    group = at.t // sz.pieces
    member = at.t - group * sz.pieces
    per = TP // sz.pieces
    for k in range(sz.heads):
        head = (member * sz.heads + k) * per + group
        lanes = tile(head, HD)

        def biased(i, k=k, lanes=lanes):
            rows = tile(i, 256)
            for which in range(3):
                cols = slice(which * sz.cols + k * HD, which * sz.cols + (k + 1) * HD)
                value = acc[rows, cols]
                if which != 1:
                    value = value + vec[which // 2 : which // 2 + 1, lanes]
                qkv[rows, cols] = value.astype(BF16)

        loop(sz.rows_all // 256, biased)
    net.keep(wq, wqkv)
    net.keep(qkv, qkv_all)

    def attend(k):
        q_cols = slice(k * HD, (k + 1) * HD)
        k_cols = slice(sz.cols + k * HD, sz.cols + (k + 1) * HD)
        v_cols = slice(2 * sz.cols + k * HD, 2 * sz.cols + (k + 1) * HD)

        def body(i):
            rows = tile(i, 256)
            scores = dot_nt(qkv[rows, q_cols], qkv[:, k_cols]) * SCALE
            top = jnp.max(scores, axis=1, keepdims=True)
            exps = jnp.exp(scores - top)
            probs = exps * (1.0 / jnp.sum(exps, axis=1, keepdims=True))
            ctx[rows, q_cols] = dot(probs.astype(BF16), qkv[:, v_cols]).astype(BF16)

        loop(sz.rows_all // 256, body)

    attend(0)
    wo_spread.relay()
    for item in wu_spread[:1]:
        item.relay()
    for k in range(1, sz.heads):
        attend(k)
    wd_chunk = rf // 4
    wd_spread = [
        Spread(net, at, lambda p, j=j: w_down.at[pl.ds(p * rf + j * wd_chunk, wd_chunk), :], at.p, at.pz)
        for j in range(4)
    ]
    net.keep(ctx, ctx_all)

    wo_spread.near()
    wo_spread.far()

    def wo_rows(k, piece):
        return pl.ds((k * sz.pieces + piece) * rw, rw)

    for k in range(sz.heads):
        net.local(wo_got.at[member * sz.heads + k], wo.at[wo_rows(k, member), :]).wait()
    wo_in = []
    for f in range(1, sz.pieces):
        other = at.index_of(f) - group * sz.pieces
        for k in range(sz.heads):
            wo_in.append(
                net.remote(wo_got.at[other * sz.heads + k], wo.at[wo_rows(k, member), :], at.peer(f))
            )
    for copy in wo_in:
        copy.wait_recv()
    net.keep(wo, w_out_own)

    sums = Scatter(net, at, sz, sum_bufs)
    for slot in (3, 1, 2, 0):
        rows = pl.ds(slot * 2 * t, 2 * t)

        def body(i, rows=rows, slot=slot):
            cols = tile(i, 512)
            sums.put(slot, cols, dot(ctx[rows, :], wo[:, cols]))

        loop(d // 512, body)
        sums.share(slot)
        if slot == 3:
            sums.send_diag()
    sums.send_free()
    for item in wu_spread[1:2]:
        item.relay()
    sums.send_joined()
    for item in wu_spread[2:3]:
        item.relay()
    sums.wait()

    def norm(i):
        rows = tile(i, STRIP)
        value = xs[rows, :].astype(F32) + sums.total(i) + vec[2:3, :]
        fin[rows, :] = value
        xhat, _ = normed(value)
        first[rows, :] = (xhat * vec[3:4, :] + vec[4:5, :]).astype(BF16)

    loop(t // STRIP, norm)
    net.keep(fin, first_in)
    net.local(first, first_all.at[pl.ds(0, t), :]).wait()
    firsts = Gather(net, at, sz, first_all, 0, t)
    firsts.send()
    for item in wu_spread[3:]:
        item.relay()
    firsts.relay()
    firsts.relay_last()
    for slot in range(4):
        firsts.ready(slot)
    for item in wd_spread:
        item.relay()
    for item in wu_spread + wd_spread:
        item.near()
        item.far()
    net.finish()


def attention_forward(sz, xin, wqkv_pack, wup_pack, wout, wdown, vec_pack):
    t, d, r = sz.tokens, sz.width, sz.rows_all
    shape = jax.ShapeDtypeStruct
    anywhere = pl.BlockSpec(memory_space=pl.ANY)
    outs = (
        shape((r, d), BF16),
        shape((d, 3 * sz.cols), BF16),
        shape((sz.cols, d), BF16),
        shape((d, sz.hid), BF16),
        shape((sz.hid, d), BF16),
        shape((8, d), F32),
        shape((8, sz.hid), F32),
        shape((r, 3 * sz.cols), BF16),
        shape((r, sz.cols), BF16),
        shape((t, d), F32),
        shape((r, d), BF16),
    )
    scratch = [
        pltpu.VMEM((r, d), BF16),
        pltpu.VMEM((d, 3 * sz.cols), BF16),
        pltpu.VMEM((sz.parts, sz.row_shard, d), BF16),
        pltpu.VMEM((sz.cols, d), BF16),
        pltpu.VMEM((sz.parts * TP, 16, HD), F32),
        pltpu.VMEM((8, d), F32),
        pltpu.VMEM((8, sz.hid), F32),
        pltpu.VMEM((r, 3 * sz.cols), F32),
        pltpu.VMEM((r, 3 * sz.cols), BF16),
        pltpu.VMEM((r, sz.cols), BF16),
        pltpu.VMEM((t, d), F32),
        pltpu.VMEM((t, d), BF16),
        *Scatter.scratch(sz),
        pltpu.SemaphoreType.DMA((80 + 28 * sz.nx,)),
        pltpu.SemaphoreType.DMA((80 + 28 * sz.nx,)),
        pltpu.SemaphoreType.DMA((24,)),
    ]
    return pl.pallas_call(
        functools.partial(attention_forward_kernel, sz),
        out_shape=outs,
        in_specs=[anywhere] * 6,
        out_specs=[anywhere] * len(outs),
        scratch_shapes=scratch,
        compiler_params=pltpu.CompilerParams(
            collective_id=0, has_side_effects=True, vmem_limit_bytes=VMEM_LIMIT
        ),
        name="attention_forward",
    )(xin, wqkv_pack, wup_pack, wout, wdown, vec_pack)


GELU_A = 0.7978845608028654
GELU_B = 0.044715


def gate(values):
    inner = jnp.tanh(GELU_A * (values + GELU_B * values * values * values))
    return 0.5 * values * (1.0 + inner)


def gate_slope(values):
    square = values * values
    inner = jnp.tanh(GELU_A * (values + GELU_B * square * values))
    rise = GELU_A * (1.0 + 3.0 * GELU_B * square)
    return 0.5 * (1.0 + inner) + 0.5 * values * (1.0 - inner * inner) * rise


def feed_forward_kernel(
    sz,
    first_all, first_in, w_up, w_down, vec_all, bup_all, cot_in,
    outputs, grad_first_in, grad_low, grad_w_up, grad_w_down, grad_vec,
    fa, wu, wd, vec, bup, fin, cot, hid, act, gh, g2, g2s, out, gv, dwu, dwd, *rest,
):
    *sum_bufs, send, recv, local = rest
    at = Place(sz)
    net = Copies(send, recv, local)
    t, d, h = sz.tokens, sz.width, sz.half
    two = 2 * t
    loads = {slot: net.local(first_all.at[pl.ds(slot * two, two), :], fa.at[pl.ds(slot * two, two), :])
             for slot in (3,)}
    load_up = net.local(w_up, wu)
    load_bup = net.local(bup_all, bup)
    for slot in (1, 2, 0):
        loads[slot] = net.local(
            first_all.at[pl.ds(slot * two, two), :], fa.at[pl.ds(slot * two, two), :]
        )
    load_down = net.local(w_down, wd)
    load_vec = net.local(vec_all, vec)
    load_fin = net.local(first_in, fin)
    own_rows = pl.ds(at.zh * h, h)
    load_cot = net.local(cot_in.at[at.zh], cot.at[own_rows, :])
    greet([at.to_c, at.to_y, at.to_z, at.to_h])
    cot_far = net.remote(cot_in.at[1 - at.zh], cot.at[own_rows, :], at.to_h)
    gv[...] = jnp.zeros_like(gv)

    sums = Scatter(net, at, sz, sum_bufs)
    load_up.wait()
    load_bup.wait()
    for slot in (3, 1, 2, 0):
        loads[slot].wait()
        rows = pl.ds(slot * two, two)

        def up(i, rows=rows):
            cols = tile(i, 512)
            value = dot(fa[rows, :], wu[:, cols]) + bup[0:1, cols]
            hid[rows, cols] = value
            act[rows, cols] = gate(value).astype(BF16)

        loop(sz.hid // 512, up)
        if slot == 3:
            load_down.wait()

        def down(i, rows=rows, slot=slot):
            cols = tile(i, 512)
            sums.put(slot, cols, dot(act[rows, :], wd[:, cols]))

        loop(d // 512, down)
        sums.share(slot)
        if slot == 1:
            sums.send_diag()
    sums.send_free()
    sums.send_joined()
    load_vec.wait()
    load_fin.wait()
    load_cot.wait()
    cot_far.wait_recv()
    sums.wait()

    def strip_sum(row, value):
        gv[row : row + 1, :] = gv[row : row + 1, :] + jnp.sum(value, axis=0, keepdims=True)

    def second_norm(i):
        rows = tile(i, STRIP)
        xhat, _ = normed(fin[rows, :])
        value = xhat * vec[3:4, :] + vec[4:5, :] + sums.total(i) + vec[5:6, :]
        xhat, scale = normed(value)
        out[rows, :] = (xhat * vec[6:7, :] + vec[7:8, :]).astype(BF16)
        grad = cot[rows, :].astype(F32)
        strip_sum(6, grad * xhat)
        strip_sum(7, grad)
        grad = normed_back(grad * vec[6:7, :], xhat, scale)
        g2s[rows, :] = grad
        low = grad.astype(BF16)
        g2[rows, :] = low
        strip_sum(5, low.astype(F32))

    loop(t // STRIP, second_norm)
    gather = Gather(net, at, sz, g2, 0, t)
    gather.send()
    net.keep(out.at[own_rows, :], outputs.at[at.zh])
    out_far = net.remote(out.at[pl.ds((1 - at.zh) * h, h), :], outputs.at[at.zh], at.to_h)
    sums.settle()

    def back(slot):
        gather.ready(slot)
        rows = pl.ds(slot * two, two)

        def down(i):
            cols = tile(i, 512)
            value = dot_nt(g2[rows, :], wd[cols, :])
            gh[rows, cols] = (value * gate_slope(hid[rows, cols])).astype(BF16)

        loop(sz.hid // 512, down)

        def up(i):
            cols = tile(i, 512)
            sums.put(slot, cols, dot_nt(gh[rows, :], wu[cols, :]))

        loop(d // 512, up)
        sums.share(slot)

    back(0)
    gather.relay()
    back(1)
    back(2)
    sums.send_free()
    gather.relay_last()
    back(3)
    sums.send_diag()

    def down_grad(i):
        rows, cols = tile(i // (d // 512), 512), tile(i % (d // 512), 512)
        dwd[rows, cols] = dot_tn(act[:, rows], g2[:, cols]).astype(BF16)

    loop((sz.hid // 512) * (d // 512), down_grad)
    net.keep(dwd, grad_w_down)
    sums.send_joined()

    def up_grad(i):
        rows, cols = tile(i // (sz.hid // 512), 512), tile(i % (sz.hid // 512), 512)
        dwu[rows, cols] = dot_tn(fa[:, rows], gh[:, cols]).astype(BF16)

    loop((sz.hid // 512) * (d // 512), up_grad)
    net.keep(dwu, grad_w_up)
    for p in range(sz.parts):
        rf = sz.hid_shard
        gv[8:9, p * sz.slab : p * sz.slab + rf] = jnp.sum(
            gh[:, p * rf : (p + 1) * rf].astype(F32), axis=0, keepdims=True
        )
    sums.wait()

    def first_norm(i):
        rows = tile(i, STRIP)
        xhat, scale = normed(fin[rows, :])
        grad = g2s[rows, :] + sums.total(i)
        strip_sum(3, grad * xhat)
        strip_sum(4, grad)
        grad = normed_back(grad * vec[3:4, :], xhat, scale)
        g2s[rows, :] = grad
        low = grad.astype(BF16)
        out_low[rows, :] = low
        strip_sum(2, low.astype(F32))

    out_low = cot
    loop(t // STRIP, first_norm)
    net.keep(g2s, grad_first_in)
    net.keep(out_low, grad_low)
    net.keep(gv, grad_vec)
    out_far.wait_recv()
    net.finish()


def feed_forward(sz, *args):
    t, d, r = sz.tokens, sz.width, sz.rows_all
    shape = jax.ShapeDtypeStruct
    anywhere = pl.BlockSpec(memory_space=pl.ANY)
    outs = (
        shape((2, sz.half, d), BF16),
        shape((t, d), F32),
        shape((t, d), BF16),
        shape((d, sz.hid), BF16),
        shape((sz.hid, d), BF16),
        shape((16, d), F32),
    )
    scratch = [
        pltpu.VMEM((r, d), BF16),
        pltpu.VMEM((d, sz.hid), BF16),
        pltpu.VMEM((sz.hid, d), BF16),
        pltpu.VMEM((8, d), F32),
        pltpu.VMEM((8, sz.hid), F32),
        pltpu.VMEM((t, d), F32),
        pltpu.VMEM((t, d), BF16),
        pltpu.VMEM((r, sz.hid), F32),
        pltpu.VMEM((r, sz.hid), BF16),
        pltpu.VMEM((r, sz.hid), BF16),
        pltpu.VMEM((r, d), BF16),
        pltpu.VMEM((t, d), F32),
        pltpu.VMEM((t, d), BF16),
        pltpu.VMEM((16, d), F32),
        pltpu.VMEM((d, sz.hid), BF16),
        pltpu.VMEM((sz.hid, d), BF16),
        *Scatter.scratch(sz),
        pltpu.SemaphoreType.DMA((40,)),
        pltpu.SemaphoreType.DMA((40,)),
        pltpu.SemaphoreType.DMA((24,)),
    ]
    return pl.pallas_call(
        functools.partial(feed_forward_kernel, sz),
        out_shape=outs,
        in_specs=[anywhere] * 7,
        out_specs=[anywhere] * len(outs),
        scratch_shapes=scratch,
        compiler_params=pltpu.CompilerParams(
            collective_id=1, has_side_effects=True, vmem_limit_bytes=VMEM_LIMIT
        ),
        name="feed_forward",
    )(*args)


class Reduce:
    def __init__(self, net, at, view, bufs, chunks, held, result):
        self.net, self.at, self.view, self.chunks = net, at, view, chunks
        self.got, self.own, self.out, self.inn = bufs
        self.rows = self.out.shape[0] // chunks
        self.result = result
        self.held = held
        self.groups = (at.x * 2 + (1 - at.zh), at.x * 2 + at.zh)

    @staticmethod
    def scratch(sz, rows, cols, dtype, held):
        return [
            pltpu.VMEM((sz.nx - 1, 2, rows, cols), dtype),
            pltpu.VMEM((2, 8, 128) if held else (2, rows, cols), dtype),
            pltpu.VMEM((rows, cols), dtype),
            pltpu.VMEM((rows, cols), dtype),
        ]

    def chunk(self, j):
        return pl.ds(j * self.rows, self.rows)

    def start(self):
        at, net = self.at, self.net
        self.from_x = {}
        for which in (0, 1):
            zh = 1 - at.zh if which == 0 else at.zh
            for j in range(self.chunks):
                for step in range(1, at.nx):
                    p = at.x_of(step) * 2 + zh
                    self.from_x[which, j, step] = net.remote(
                        self.view(p, j), self.got.at[step - 1, which, self.chunk(j), :], at.to_x(step)
                    )
        if not self.held:
            self.loads = {
                (which, j): net.local(self.view(self.groups[which], j), self.own.at[which, self.chunk(j), :])
                for which in (0, 1)
                for j in range(self.chunks)
            }
        self.from_h = {}

    def term(self, which, j, i):
        rows = pl.ds(pl.multiple_of(j * self.rows + i * STRIP, STRIP), STRIP)
        if self.held:
            total = self.view(self.groups[which], j)[tile(i, STRIP), :].astype(F32)
        else:
            total = self.own[which, rows, :].astype(F32)
        for step in range(1, self.at.nx):
            total = total + self.got[step - 1, which, rows, :].astype(F32)
        return rows, total

    def ready(self, which, j):
        for step in range(1, self.at.nx):
            self.from_x[which, j, step].wait_recv()
        if not self.held:
            self.loads[which, j].wait()

    def hop(self, j):
        self.ready(0, j)

        def body(i):
            rows, total = self.term(0, j, i)
            self.out[rows, :] = total.astype(self.out.dtype)

        loop(self.rows // STRIP, body)
        self.from_h[j] = self.net.remote(
            self.out.at[self.chunk(j), :], self.inn.at[self.chunk(j), :], self.at.to_h
        )

    def close(self, j):
        self.ready(1, j)
        self.from_h[j].wait_recv()

        def body(i):
            rows, total = self.term(1, j, i)
            self.result[rows, :] = (total + self.inn[rows, :].astype(F32)).astype(self.result.dtype)

        loop(self.rows // STRIP, body)


def attention_backward_kernel(
    sz,
    grad_low, grad_first_in, x_all, wqkv, w_out_own, qkv_all, ctx_all, grad_w_up, grad_w_down, grad_vec,
    input_grad, out_wqkv, out_wo, out_wup, out_wdown, out_vec, out_bup,
    gb, xs, wq, wo, qkv, ctx, gfi, gv, dctx, dqkv, dk, dv, ig, dwq, dwo, dwo_own, res_q, res_o, res_u, res_d, res_v,
    vec_got, vec_sum, bup_out, *rest,
):
    *bufs, send, recv, local = rest
    sum_bufs, bufs = bufs[:7], bufs[7:]
    at = Place(sz)
    net = Copies(send, recv, local)
    t, d, h = sz.tokens, sz.width, sz.half
    two = 2 * t
    rw, rf = sz.row_shard, sz.hid_shard
    flips = range(1, TP)
    load_gb = net.local(grad_low, gb.at[pl.ds(0, t), :])
    load_wo = net.local(w_out_own, wo)
    load_qkv = net.local(qkv_all, qkv)
    load_ctx = net.local(ctx_all, ctx)
    load_gv = net.local(grad_vec, gv)
    greet([at.peer(f) for f in flips] + [at.to_h] + [at.to_x(s) for s in range(1, sz.nx)])
    load_gb.wait()
    gather = Gather(net, at, sz, gb, 0, t)
    gather.send()

    up_rows, down_rows = sz.slab // 4, rf // 4
    sum_u = Reduce(
        net, at, lambda p, j: grad_w_up.at[pl.ds(p * sz.slab + j * up_rows, up_rows), :],
        bufs[0:4], 4, False, res_u,
    )
    sum_d = Reduce(
        net, at, lambda p, j: grad_w_down.at[pl.ds(p * rf + j * down_rows, down_rows), :],
        bufs[4:8], 4, False, res_d,
    )
    sum_q = Reduce(
        net, at, lambda p, j: dwq.at[pl.ds(p * sz.slab + j * up_rows, up_rows), :], bufs[8:12], 4, True, res_q
    )
    sum_o = Reduce(net, at, lambda p, j: dwo_own.at[p], bufs[12:16], 1, True, res_o)
    sum_v = Reduce(
        net, at, lambda p, j: gv.at[:, pl.ds(pl.multiple_of(p * sz.slab, sz.slab), sz.slab)],
        bufs[16:20], 1, True, res_v,
    )
    sum_u.start()
    sum_d.start()
    load_x = net.local(x_all, xs)
    load_wq = net.local(wqkv, wq)
    load_gfi = net.local(grad_first_in, gfi)
    hops = [(s, j) for s in (sum_u, sum_d) for j in range(4)]
    closes = list(hops)

    def pump(count):
        for _ in range(min(count, len(hops))):
            item, j = hops.pop(0)
            item.hop(j)

    load_wo.wait()

    def context_grad(slot):
        gather.ready(slot)
        rows = pl.ds(slot * two, two)
        dctx[rows, :] = dot_nt(gb[rows, :], wo[...]).astype(BF16)

    context_grad(0)
    gather.relay()
    context_grad(1)
    context_grad(2)
    gather.relay_last()
    pump(1)
    context_grad(3)
    load_qkv.wait()

    def attend_back(k):
        q_cols = slice(k * HD, (k + 1) * HD)
        k_cols = slice(sz.cols + k * HD, sz.cols + (k + 1) * HD)
        v_cols = slice(2 * sz.cols + k * HD, 2 * sz.cols + (k + 1) * HD)
        turned = qkv[:, k_cols].T

        def body(i):
            rows = tile(i, 256)
            queries, grads = qkv[rows, q_cols], dctx[rows, q_cols]
            scores = dot_nt(qkv[:, k_cols], queries) * SCALE
            exps = jnp.exp(scores - jnp.max(scores, axis=0, keepdims=True))
            probs = exps * (1.0 / jnp.sum(exps, axis=0, keepdims=True))
            value_part = dot(probs.astype(BF16), grads)
            slopes = probs * dot_nt(qkv[:, v_cols], grads)
            score_grads = (slopes - probs * jnp.sum(slopes, axis=0, keepdims=True)).astype(BF16)
            key_part = dot(score_grads, queries)
            first = i == 0
            dv[...] = jnp.where(first, value_part, dv[...] + value_part)
            dk[...] = jnp.where(first, key_part, dk[...] + key_part)
            dqkv[rows, q_cols] = (dot(turned, score_grads).T * SCALE).astype(BF16)

        loop(sz.rows_all // 256, body)
        dqkv[:, k_cols] = (dk[...] * SCALE).astype(BF16)
        dqkv[:, v_cols] = dv[...].astype(BF16)

    attend_back(0)
    pump(1)
    for k in range(1, sz.heads):
        attend_back(k)
    pump(1)
    load_wq.wait()

    sums = Scatter(net, at, sz, sum_bufs)
    for slot in (3, 1, 2, 0):
        rows = pl.ds(slot * two, two)

        def body(i, rows=rows, slot=slot):
            cols = tile(i, 512)
            sums.put(slot, cols, dot_nt(dqkv[rows, :], wq[cols, :]))

        loop(d // 512, body)
        sums.share(slot)
        if slot == 1:
            sums.send_diag()
    sums.send_free()
    pump(1)
    load_x.wait()
    load_ctx.wait()

    def qkv_grad(i):
        rows = tile(i, 512)
        dwq[rows, :] = dot_tn(xs[:, rows], dqkv[...]).astype(BF16)

    loop(d // 512, qkv_grad)
    sum_q.start()
    sums.send_joined()

    def out_grad(i):
        cols = tile(i, 512)
        dwo[:, cols] = dot_tn(ctx[...], gb[:, cols]).astype(BF16)

    loop(d // 512, out_grad)
    group = at.t // sz.pieces
    member = at.t - group * sz.pieces
    per = TP // sz.pieces
    wo_in = []
    for k in range(sz.heads):
        for f in range(1, sz.pieces):
            other = at.index_of(f) - group * sz.pieces
            wo_in.append(
                net.remote(
                    dwo.at[pl.ds((k * sz.pieces + other) * rw, rw), :],
                    dwo_own.at[member * sz.heads + k],
                    at.peer(f),
                )
            )
        net.local(
            dwo.at[pl.ds((k * sz.pieces + member) * rw, rw), :], dwo_own.at[member * sz.heads + k]
        ).wait()
    load_gv.wait()
    for k in range(sz.heads):
        lanes = tile((member * sz.heads + k) * per + group, HD)
        gv[0:1, lanes] = jnp.sum(dqkv[:, k * HD : (k + 1) * HD].astype(F32), axis=0, keepdims=True)
        at_v = 2 * sz.cols + k * HD
        gv[1:2, lanes] = jnp.sum(dqkv[:, at_v : at_v + HD].astype(F32), axis=0, keepdims=True)
    for copy in wo_in:
        copy.wait_recv()
    sum_o.start()
    sum_v.start()
    load_gfi.wait()
    sums.wait()

    def final(i):
        rows = tile(i, STRIP)
        ig[rows, :] = (gfi[rows, :] + sums.total(i)).astype(BF16)

    loop(t // STRIP, final)
    pump(8)
    own_rows = pl.ds(at.zh * h, h)
    net.keep(ig.at[own_rows, :], input_grad.at[at.zh])
    ig_far = net.remote(ig.at[pl.ds((1 - at.zh) * h, h), :], input_grad.at[at.zh], at.to_h)
    for j in range(4):
        sum_q.hop(j)
    sum_o.hop(0)
    sum_v.hop(0)

    for item, j in closes:
        item.close(j)
    net.keep(res_d, out_wdown)
    net.keep(res_u.at[pl.ds(at.t * rw, rw), :], out_wup.at[at.t])
    back_in = [
        net.remote(res_u.at[pl.ds(at.index_of(f) * rw, rw), :], out_wup.at[at.t], at.peer(f)) for f in flips
    ]
    for j in range(4):
        sum_q.close(j)
    net.keep(res_q.at[pl.ds(at.t * rw, rw), :], out_wqkv.at[at.t])
    back_in += [
        net.remote(res_q.at[pl.ds(at.index_of(f) * rw, rw), :], out_wqkv.at[at.t], at.peer(f)) for f in flips
    ]
    sum_o.close(0)
    net.keep(res_o, out_wo)
    sum_v.close(0)

    def lanes_of(index):
        return pl.ds(pl.multiple_of(index // sz.pieces * HD, HD), HD)

    vec_got[at.t] = res_v[0:8, lanes_of(at.t)]
    vec_in = [
        net.remote(res_v.at[pl.ds(0, 8), lanes_of(at.index_of(f))], vec_got.at[at.t], at.peer(f)) for f in flips
    ]
    bup_out[...] = res_v[8:16, 0:rf]
    net.keep(bup_out, out_bup)
    for copy in vec_in:
        copy.wait_recv()
    total = vec_got[0]
    for member in range(1, TP):
        total = total + vec_got[member]
    vec_sum[...] = total
    net.keep(vec_sum, out_vec)
    for copy in back_in:
        copy.wait_recv()
    ig_far.wait_recv()
    net.finish()


def attention_backward(sz, *args):
    t, d, r = sz.tokens, sz.width, sz.rows_all
    rw, rf = sz.row_shard, sz.hid_shard
    wide = 3 * sz.cols
    shape = jax.ShapeDtypeStruct
    anywhere = pl.BlockSpec(memory_space=pl.ANY)
    outs = (
        shape((2, sz.half, d), BF16),
        shape((TP, rw, wide), BF16),
        shape((rw, d), BF16),
        shape((TP, rw, sz.hid), BF16),
        shape((rf, d), BF16),
        shape((8, HD), F32),
        shape((8, rf), F32),
    )
    scratch = [
        pltpu.VMEM((r, d), BF16),
        pltpu.VMEM((r, d), BF16),
        pltpu.VMEM((d, wide), BF16),
        pltpu.VMEM((sz.cols, d), BF16),
        pltpu.VMEM((r, wide), BF16),
        pltpu.VMEM((r, sz.cols), BF16),
        pltpu.VMEM((t, d), F32),
        pltpu.VMEM((16, d), F32),
        pltpu.VMEM((r, sz.cols), BF16),
        pltpu.VMEM((r, wide), BF16),
        pltpu.VMEM((r, HD), F32),
        pltpu.VMEM((r, HD), F32),
        pltpu.VMEM((t, d), BF16),
        pltpu.VMEM((d, wide), BF16),
        pltpu.VMEM((sz.cols, d), BF16),
        pltpu.VMEM((sz.parts, rw, d), BF16),
        pltpu.VMEM((sz.slab, wide), BF16),
        pltpu.VMEM((rw, d), BF16),
        pltpu.VMEM((sz.slab, sz.hid), BF16),
        pltpu.VMEM((rf, d), BF16),
        pltpu.VMEM((16, sz.slab), F32),
        pltpu.VMEM((TP, 8, HD), F32),
        pltpu.VMEM((8, HD), F32),
        pltpu.VMEM((8, rf), F32),
        *Scatter.scratch(sz),
        *Reduce.scratch(sz, sz.slab, sz.hid, BF16, False),
        *Reduce.scratch(sz, rf, d, BF16, False),
        *Reduce.scratch(sz, sz.slab, wide, BF16, True),
        *Reduce.scratch(sz, rw, d, BF16, True),
        *Reduce.scratch(sz, 16, sz.slab, F32, True),
        pltpu.SemaphoreType.DMA((70 + 28 * sz.nx,)),
        pltpu.SemaphoreType.DMA((70 + 28 * sz.nx,)),
        pltpu.SemaphoreType.DMA((48,)),
    ]
    return pl.pallas_call(
        functools.partial(attention_backward_kernel, sz),
        out_shape=outs,
        in_specs=[anywhere] * 10,
        out_specs=[anywhere] * len(outs),
        scratch_shapes=scratch,
        compiler_params=pltpu.CompilerParams(
            collective_id=2, has_side_effects=True, vmem_limit_bytes=VMEM_LIMIT
        ),
        name="attention_backward",
    )(*args)


def per_device(
    sz, inputs, cotangent, w_query, w_key, w_value, w_out, b_query, b_value, b_out, ln1_gain, ln1_bias,
    w_up, b_up, w_down, b_down, ln2_gain, ln2_bias,
):
    rw, rf, d = sz.row_shard, sz.hid_shard, sz.width
    groups = TP // sz.pieces
    t = lax.axis_index("zl") * 4 + lax.axis_index("y") * 2 + lax.axis_index("c")
    p = lax.axis_index("x") * 2 + lax.axis_index("zh")

    def by_member(weight):
        split = weight.reshape(rw, sz.pieces, sz.heads, groups, HD)
        return split.transpose(3, 1, 0, 2, 4).reshape(TP, rw, sz.cols)

    wqkv_pack = jnp.concatenate([by_member(w) for w in (w_query, w_key, w_value)], axis=2)
    wup_pack = w_up.reshape(rw, sz.parts, TP, rf).transpose(2, 0, 1, 3).reshape(TP, rw, sz.hid)
    rows = jnp.stack(
        [v.astype(F32) for v in (b_query, b_value, b_out, ln1_gain, ln1_bias, b_down, ln2_gain, ln2_bias)]
    )
    low = lax.dynamic_update_slice(jnp.zeros((8, HD), F32), rows, (0, (t % sz.pieces) * rw))
    up = b_up.astype(F32)
    if rf >= HD:
        high = jnp.zeros((8, HD), F32).at[: rf // HD].set(up.reshape(rf // HD, HD))
    else:
        high = lax.dynamic_update_slice(
            jnp.zeros((8, HD), F32), up[None], (0, (p % (HD // rf)) * rf)
        )
    vec_pack = jnp.concatenate([low, high], axis=0)

    x_all, wqkv, w_out_own, up_own, down_own, vec_all, bup_all, qkv, ctx, first_in, first_all = attention_forward(
        sz, inputs, wqkv_pack, wup_pack, w_out, w_down, vec_pack
    )
    outputs, grad_first_in, grad_low, grad_up, grad_down, grad_vec = feed_forward(
        sz, first_all, first_in, up_own, down_own, vec_all, bup_all, cotangent
    )
    input_grad, out_wqkv, out_wo, out_wup, out_wdown, out_vec, out_bup = attention_backward(
        sz, grad_low, grad_first_in, x_all, wqkv, w_out_own, qkv, ctx, grad_up, grad_down, grad_vec
    )

    def by_rows(which):
        part = out_wqkv[:, :, which * sz.cols : (which + 1) * sz.cols]
        split = part.reshape(groups, sz.pieces, rw, sz.heads, HD)
        return split.transpose(2, 1, 3, 0, 4).reshape(rw, d).astype(F32)

    grad_wup = out_wup.reshape(TP, rw, sz.parts, rf).transpose(1, 2, 0, 3).reshape(rw, sz.hidden)
    vec = lax.dynamic_slice(out_vec, (0, (t % sz.pieces) * rw), (8, rw))
    return (
        outputs,
        input_grad.astype(F32),
        by_rows(0),
        by_rows(1),
        by_rows(2),
        out_wo.astype(F32),
        vec[0],
        vec[1],
        vec[2],
        vec[3],
        vec[4],
        grad_wup.astype(F32),
        out_bup[0],
        out_wdown.astype(F32),
        vec[5],
        vec[6],
        vec[7],
    )


def solution(mesh):
    nx = mesh.shape["dp"]
    plane = Mesh(mesh.devices.reshape(nx, 2, mesh.shape["hd"] // 2, 2, mesh.shape["sq"] // 2), AXES)
    rows, matrix, vector = P("x", AXES[1:], None), P(AXES, None), P(AXES)

    def run(*args):
        batch, length, width = args[0].shape
        sz = Sizes(nx, width, args[11].shape[1], batch // nx * length // (2 * TP))
        call = jax.shard_map(
            functools.partial(per_device, sz),
            mesh=plane,
            in_specs=(rows, rows) + (matrix,) * 4 + (vector,) * 5 + (matrix, vector, matrix) + (vector,) * 3,
            out_specs=(rows, rows) + (matrix,) * 4 + (vector,) * 5 + (matrix, vector, matrix) + (vector,) * 3,
            check_vma=False,
        )
        return call(*args)

    return run
```

time: 3360 us -> 546 us (0.16)
  waiting for transfers between devices: 2660 us -> 0 us
  Pallas kernels: 0 us -> 516 us
  matrix products: 324 us -> 0 us
  blocking collectives: 141 us -> 0 us
  local copies, waits for them, and re-layouts: 123 us -> 19.7 us
  starting transfers between devices: 59.9 us -> 0 us
    reduce_scatter x5 -> x0, waiting for transfers between devices: 1540 us -> none  [the longest x1 709 us: per_device(): lax.psum_scatter(grad_w_up, ('dp', 'hd', 'sq'), scatter_dimension=0, tile...]
    unnamed x23 -> x0, waiting for transfers between devices: 568 us -> none
    all_gather x10 -> x0, waiting for transfers between devices: 543 us -> none  [the longest x1 188 us: fetch_mlp(): lax.all_gather(w_up, ('dp', 'hd', 'sq'), axis=0, tiled=True)]
    pallas_call x0 -> x3, Pallas kernels: none -> 516 us  [the longest x1 228 us: attention_forward(): pl.pallas_call(functools.partial(attention_forward_kernel, sz), out_shape...]
    dot_general x78 -> x0, matrix products: 324 us -> none  [the longest x12 104 us: matmul_right(): lax.dot_general(left_side, right_side, (((1,), (1,)), ((), ())), preferre...]
    unnamed x165 -> x15, local copies, waits for them, and re-layouts: 73.8 us -> 3.59 us
    all_to_all x5 -> x0, blocking collectives: 62.4 us -> none  [the longest x2 26.5 us: attention_forward(): lax.all_to_all(keys_tok, 'hd', split_axis=1, concat_axis=0, tiled=True)]
    all_to_all x11 -> x0, starting transfers between devices: 58.9 us -> none  [the longest x2 15.8 us: attention_forward(): lax.all_to_all(context_rows.astype(jnp.bfloat16), 'hd', split_axis=0, con...]
  transfers between devices with their start and end apart: 30 -> 0, of which waited for: 17 -> 0; matrix products, arithmetic and copies ran while one was open for 10% -> 0% of each run, Pallas kernels for 0% -> 0%
where the time goes in v1:
time: 546 us; the launch traced here: 545 us
  Pallas kernels  516 us (95%)
  local copies, waits for them, and re-layouts  19.7 us (4%)
  other arithmetic  7.84 us (1%)
    pallas_call x1, Pallas kernels, attention_forward(): pl.pallas_call(functools.partial(attention_forward_kernel, sz), out_shape...  228 us
    pallas_call x1, Pallas kernels, attention_backward(): pl.pallas_call(functools.partial(attention_backward_kernel, sz), out_shap...  199 us
    pallas_call x1, Pallas kernels, feed_forward(): pl.pallas_call(functools.partial(feed_forward_kernel, sz), out_shape=outs...  89.7 us

profile of v1, /device:TPU:17, one launch (start us, length us, event | category | flops | bytes accessed | tf_op | source)
XLA Modules:
  0.0 544.8 jit_solution(1496557913004210687)
XLA Ops:
  0.7 0.0 copy-start.5
  0.7 0.8 stack.46
  1.5 0.7 pad_convert_fusion
  2.2 0.2 dynamic_update_slice.3
  2.4 0.6 pad_maximum_fusion.1.vec_pack
  3.0 1.1 reshape.112
  4.1 0.2 copy.51
  4.3 0.2 reshape.113
  4.5 1.1 reshape.114
  5.6 0.0 copy-start.2
  5.6 0.2 copy.50
  5.8 0.2 reshape.115
  6.0 0.0 copy-done.5
  6.0 0.2 reshape.116
  6.2 0.2 copy.49
  6.4 0.2 reshape.117
  6.6 0.9 pad_maximum_fusion.wqkv_pack
  7.5 0.0 copy-done.2
  7.5 0.3 copy.42
  7.8 0.4 copy.48
  8.2 1.5 reshape.119.wup_pack
  9.7 228.1 %attention_forward.1 = (bf16[1024,2048]{1,0:T(8,128)(2,1)}, bf16[2048,768]{1,0:T(8,128)(2,1)}, bf16[256,2048]{1,0:T(8,128)(2,1)}, bf16[2048,1024]{1,0:T(8,128)(2...) custom-call(bf16[2,64,2048]{2,1,0:T(8,128)(2,1)} %xin.1, ...), custom_call_target="tpu_custom_call" | custom-call | tf_op jit(solution)/shard_map/attention_forward/pallas_call | solution.py:605
  237.8 89.7 %feed_forward.1 = (bf16[2,64,2048]{2,1,0:T(8,128)(2,1)}, f32[128,2048]{1,0:T(8,128)}, bf16[128,2048]{1,0:T(8,128)(2,1)}, bf16[2048,1024]{1,0:T(8,128)(2,1)}, bf1...) custom-call(bf16[1024,2048]{1,0:T(8,128)(2,1)} %get-tuple-element.53.first_all, f32[128,2048]{1,0:T(8,128)} %get-tuple-element.54.first_in, ...), custom_call_target="tpu_custom_call" | custom-call | tf_op jit(solution)/shard_map/feed_forward/pallas_call | solution.py:823
  327.6 198.5 %attention_backward.1 = (bf16[2,64,2048]{2,1,0:T(8,128)(2,1)}, bf16[8,64,768]{2,1,0:T(8,128)(2,1)}, bf16[64,2048]{1,0:T(8,128)(2,1)}, bf16[8,64,1024]{2,1,0:T(8,...) custom-call(bf16[128,2048]{1,0:T(8,128)(2,1)} %get-tuple-element.60.grad_low, ...), custom_call_target="tpu_custom_call" | custom-call | tf_op jit(solution)/shard_map/attention_backward/pallas_call | solution.py:1181
  526.1 0.0 copy-start.3
  526.1 1.3 slice.60
  527.4 0.8 constant_dynamic-slice_fusion
  528.2 0.5 slice_bitcast_fusion
  528.7 2.1 convert_element_type.66
  530.9 1.8 convert_element_type.79
  532.6 0.0 copy-done.3
  532.6 0.2 slice_convert_fusion
  532.8 0.3 reshape.127
  533.1 0.3 copy.40
  533.4 1.0 reshape.123
  534.5 0.3 reshape.126
  534.7 0.3 copy.39
  535.1 0.0 copy-start.1
  535.1 1.0 reshape.122
  536.1 0.3 reshape.125
  536.4 0.3 copy.38
  536.7 1.0 reshape.121
  537.7 0.0 copy-done.1
  537.7 0.9 reshape.128
  538.7 1.2 copy.41
  539.9 0.0 copy-start
  539.9 2.5 copy.43
  542.4 0.0 copy-start.4
  542.4 0.0 copy-done
  542.4 1.6 convert_element_type.84
  544.0 0.0 copy-done.4
  544.0 0.8 copy.54
  (2 shorter events, 0.0 us)
Async XLA Ops:
  0.7 5.3 copy-start.5
  5.6 1.9 copy-start.2
  526.1 6.5 %copy-start.3 = (bf16[8,64,768]{2,1,0:T(8,128)(2,1)S(1)}, bf16[8,64,768]{2,1,0:T(8,128)(2,1)}, u32[]{:S(2)}) copy-start(bf16[8,64,768]{2,1,0:T(8,128)(2,1)} %get-tuple-element.71) | copy-start | bytes 2359300
  535.1 2.6 copy-start.1
  539.9 2.5 copy-start
  542.4 1.6 copy-start.4

commit v2 on v1

--- a/solution.py
+++ b/solution.py
@@ -163,9 +163,9 @@
 
 
 class Gather:
-    def __init__(self, net, at, sz, buf, start, count):
+    def __init__(self, net, at, sz, buf, start, count, tall=False):
         self.net, self.at, self.sz, self.buf = net, at, sz, buf
-        self.start, self.count = start, count
+        self.start, self.count, self.tall = start, count, tall
         half = sz.width // 2
         self.cols = (pl.ds(0, half), pl.ds(half, half))
         self.sib = [None] * 4
@@ -192,6 +192,21 @@
 
     def relay(self):
         net, at = self.net, self.at
+        if self.tall:
+            to_y = []
+            for h in (1, 0):
+                self.from_z[h].wait_recv()
+                to_y.append(
+                    net.remote(
+                        self.part(2, 0, self.cols[h]), self.part(3, 0, self.cols[h]), at.to_y
+                    )
+                )
+            self.diag = tuple(to_y)
+            self.share(2)
+            for copy in self.from_y:
+                copy.wait_recv()
+            self.share(1)
+            return
         self.from_y[0].wait_recv()
         to_z = net.remote(
             self.part(1, 0, self.cols[0]), self.part(3, 0, self.cols[0]), at.to_z
@@ -216,8 +231,8 @@
 
 
 class Scatter:
-    def __init__(self, net, at, sz, bufs):
-        self.net, self.at, self.sz = net, at, sz
+    def __init__(self, net, at, sz, bufs, tall=False):
+        self.net, self.at, self.sz, self.tall = net, at, sz, tall
         self.mine, self.theirs, self.got, self.diag, self.diag_got, self.out, self.inn = bufs
         self.sib = [None] * 4
 
@@ -262,7 +277,9 @@
         self.add(3, 0, 2 * h, self.diag, 0)
         low, high = pl.ds(0, h), pl.ds(h, h)
         self.d_low = net.remote(self.diag.at[low, :], self.diag_got.at[low, :], at.to_y)
-        self.d_high = net.remote(self.diag.at[high, :], self.diag_got.at[high, :], at.to_z)
+        self.d_high = net.remote(
+            self.diag.at[high, :], self.diag_got.at[high, :], at.to_y if self.tall else at.to_z
+        )
 
     def half_out(self, side, start, target):
         rows = pl.ds(side * self.sz.tokens + start, self.sz.half)
@@ -273,12 +290,25 @@
         self.sib[1].wait_recv()
         self.add(1, 0, h, self.out, 0)
         self.y_low = self.half_out(0, 0, at.to_y)
+        if self.tall:
+            self.add(1, h, h, self.out, h)
+            self.y_high = self.half_out(0, h, at.to_y)
+            return
         self.sib[2].wait_recv()
         self.add(2, h, h, self.out, t + h)
         self.z_high = self.half_out(1, h, at.to_z)
 
     def send_joined(self):
         at, t, h = self.at, self.sz.tokens, self.sz.half
+        if self.tall:
+            self.sib[2].wait_recv()
+            self.d_low.wait_recv()
+            self.add(2, 0, h, self.out, t, self.diag_got)
+            self.z_low = self.half_out(1, 0, at.to_z)
+            self.d_high.wait_recv()
+            self.add(2, h, h, self.out, t + h, self.diag_got)
+            self.z_high = self.half_out(1, h, at.to_z)
+            return
         self.d_high.wait_recv()
         self.add(1, h, h, self.out, h, self.diag_got)
         self.y_high = self.half_out(0, h, at.to_y)
@@ -308,20 +338,25 @@
 
 
 class Spread:
-    def __init__(self, net, at, view, own, across):
+    def __init__(self, net, at, view, source=None):
         self.net, self.at, self.view = net, at, view
-        self.own, self.across = own, across
-        self.from_h = net.remote(view(own), view(own), at.to_h)
+        self.source = view(at.p) if source is None else source
+        self.relayed = []
+
+    def across(self):
+        self.from_h = self.net.remote(self.source, self.view(self.at.p), self.at.to_h)
+
+    def along(self):
         self.from_x = [
-            net.remote(view(own), view(own), at.to_x(step)) for step in range(1, at.nx)
+            self.net.remote(self.source, self.view(self.at.p), self.at.to_x(step))
+            for step in range(1, self.at.nx)
         ]
-        self.relayed = []
 
     def relay(self):
         self.from_h.wait_recv()
+        there = self.view(self.at.pz)
         self.relayed = [
-            self.net.remote(self.view(self.across), self.view(self.across), self.at.to_x(step))
-            for step in range(1, self.at.nx)
+            self.net.remote(there, there, self.at.to_x(step)) for step in range(1, self.at.nx)
         ]
 
     def near(self):
@@ -336,8 +371,8 @@
 def attention_forward_kernel(
     sz,
     xin, wqkv_pack, wup_pack, wout, wdown, vec_pack,
-    x_all, wqkv, w_out_own, w_up, w_down, vec_all, bup_all, qkv_all, ctx_all, first_in, first_all,
-    xs, wq, wo_got, wo, vecs, vec, bup, acc, qkv, ctx, fin, first, *rest,
+    x_all, wqkv, w_out_own, w_up, w_down, vec_all, bup_all, qkv_all, ctx_all, first_in, first_low,
+    xs, wq, wo_got, wo, vecs, vec, bup, acc, qkv, ctx, fin, first, wu_own, wd_own, *rest,
 ):
     *sum_bufs, send, recv, local = rest
     at = Place(sz)
@@ -358,48 +393,58 @@
 
     own_wq = net.local(wqkv_pack.at[at.t], wq.at[wq_rows(at.p, at.t), :])
     own_vec = net.local(vec_pack, vecs.at[at.p * TP + at.t])
-    own_wu = net.local(wup_pack.at[at.t], w_up.at[wq_rows(at.p, at.t), :])
-    own_wd = net.local(wdown, w_down.at[pl.ds(at.p * rf, rf), :])
     own_wo = net.local(wout, wo_got.at[at.p])
-    vec_in = [net.remote(vec_pack, vecs.at[at.p * TP + at.t], at.peer(f)) for f in flips]
+    wu_here = net.local(wup_pack.at[at.t], wu_own)
+    wd_here = net.local(wdown.at[pl.ds(0, rf // 2), :], wd_own)
     wq_in = [None] + [
         net.remote(wqkv_pack.at[at.index_of(f)], wq.at[wq_rows(at.p, at.t), :], at.peer(f))
         for f in flips
     ]
+    vec_in = [net.remote(vec_pack, vecs.at[at.p * TP + at.t], at.peer(f)) for f in flips]
     own_x.wait()
-    near_rows = Gather(net, at, sz, xs, at.zh * h, h)
+    near_rows = Gather(net, at, sz, xs, at.zh * h, h, tall=True)
     near_rows.send()
 
     def chip_block(buf, f):
         member = at.index_of(f) - at.c
         return lambda p: buf.at[wq_rows(p, member, 2), :]
 
-    wq_spread = []
-    for f in (0, 2, 4, 6):
+    wq_spread = [Spread(net, at, chip_block(wq, f)) for f in (0, 2, 4, 6)]
+    for f, item in zip((0, 2, 4, 6), wq_spread):
         if f == 0:
             own_wq.wait()
         else:
             wq_in[f].wait_recv()
         wq_in[f + 1].wait_recv()
-        wq_spread.append(Spread(net, at, chip_block(wq, f), at.p, at.pz))
+        item.across()
+        item.along()
     own_vec.wait()
     for copy in vec_in:
         copy.wait_recv()
-    vec_spread = Spread(net, at, lambda p: vecs.at[pl.ds(p * TP, TP)], at.p, at.pz)
+    vec_spread = Spread(net, at, lambda p: vecs.at[pl.ds(p * TP, TP)])
+    wo_spread = Spread(net, at, lambda p: wo_got.at[p], wout)
+    vec_spread.across()
+    vec_spread.along()
+    wo_spread.along()
+    from_h.wait_recv()
+    far_rows = Gather(net, at, sz, xs, (1 - at.zh) * h, h, tall=True)
+    far_rows.send()
+    near_rows.relay()
+    far_rows.relay()
+    wq_spread[0].relay()
+    near_rows.relay_last()
+    far_rows.relay_last()
+    vec_spread.relay()
+    wq_spread[1].relay()
+    wo_spread.across()
+    wu_here.wait()
+    own_wu = net.local(wu_own, w_up.at[wq_rows(at.p, at.t), :])
+    wd_here.wait()
+    net.keep(wd_own, w_down.at[pl.ds(at.p * (rf // 2), rf // 2), :])
     wu_in = [None] + [
         net.remote(wup_pack.at[at.index_of(f)], w_up.at[wq_rows(at.p, at.t), :], at.peer(f))
         for f in flips
     ]
-    from_h.wait_recv()
-    far_rows = Gather(net, at, sz, xs, (1 - at.zh) * h, h)
-    far_rows.send()
-    near_rows.relay()
-    own_wo.wait()
-    wo_spread = Spread(net, at, lambda p: wo_got.at[p], at.p, at.pz)
-    vec_spread.relay()
-    far_rows.relay()
-    near_rows.relay_last()
-    far_rows.relay_last()
 
     def accumulate(zh, first_part):
         def body(i):
@@ -419,18 +464,20 @@
         item.near()
     net.keep(xs, x_all)
     accumulate(at.zh, True)
-    for item in wq_spread:
+    for item in wq_spread[2:]:
         item.relay()
-    own_wu.wait()
-    own_wd.wait()
-    wu_spread = []
-    for f in (0, 2, 4, 6):
-        if f:
-            wu_in[f].wait_recv()
-        wu_in[f + 1].wait_recv()
-        wu_spread.append(Spread(net, at, chip_block(w_up, f), at.p, at.pz))
-    for item in wq_spread:
-        item.far()
+    wd_chunk = rf // 4
+    wd_spread = [
+        Spread(
+            net,
+            at,
+            lambda p, j=j: w_down.at[pl.ds(p * 2 * wd_chunk + j * wd_chunk, wd_chunk), :],
+            wdown.at[pl.ds(j * wd_chunk, wd_chunk), :],
+        )
+        for j in range(2)
+    ]
+    for item in wd_spread:
+        item.across()
     vec_spread.near()
     vec_spread.far()
     for j in range(d // HD):
@@ -452,7 +499,12 @@
             bup[0:1, j * HD : (j + 1) * HD] = row
     net.keep(vec, vec_all)
     net.keep(bup, bup_all)
+    for item in wq_spread:
+        item.far()
     accumulate(1 - at.zh, False)
+    wo_spread.relay()
+    for item in wd_spread:
+        item.along()
 
     group = at.t // sz.pieces
     member = at.t - group * sz.pieces
@@ -489,19 +541,11 @@
 
         loop(sz.rows_all // 256, body)
 
-    attend(0)
-    wo_spread.relay()
-    for item in wu_spread[:1]:
-        item.relay()
-    for k in range(1, sz.heads):
+    for k in range(sz.heads):
         attend(k)
-    wd_chunk = rf // 4
-    wd_spread = [
-        Spread(net, at, lambda p, j=j: w_down.at[pl.ds(p * rf + j * wd_chunk, wd_chunk), :], at.p, at.pz)
-        for j in range(4)
-    ]
     net.keep(ctx, ctx_all)
 
+    own_wo.wait()
     wo_spread.near()
     wo_spread.far()
 
@@ -520,8 +564,17 @@
     for copy in wo_in:
         copy.wait_recv()
     net.keep(wo, w_out_own)
-
-    sums = Scatter(net, at, sz, sum_bufs)
+    wu_spread = [Spread(net, at, chip_block(w_up, f)) for f in (0, 2, 4, 6)]
+    own_wu.wait()
+    for f, item in zip((0, 2, 4, 6), wu_spread):
+        if f:
+            wu_in[f].wait_recv()
+        wu_in[f + 1].wait_recv()
+        item.across()
+    for item in wu_spread:
+        item.along()
+
+    sums = Scatter(net, at, sz, sum_bufs, tall=True)
     for slot in (3, 1, 2, 0):
         rows = pl.ds(slot * 2 * t, 2 * t)
 
@@ -534,10 +587,8 @@
         if slot == 3:
             sums.send_diag()
     sums.send_free()
-    for item in wu_spread[1:2]:
-        item.relay()
     sums.send_joined()
-    for item in wu_spread[2:3]:
+    for item in wd_spread:
         item.relay()
     sums.wait()
 
@@ -550,16 +601,8 @@
 
     loop(t // STRIP, norm)
     net.keep(fin, first_in)
-    net.local(first, first_all.at[pl.ds(0, t), :]).wait()
-    firsts = Gather(net, at, sz, first_all, 0, t)
-    firsts.send()
-    for item in wu_spread[3:]:
-        item.relay()
-    firsts.relay()
-    firsts.relay_last()
-    for slot in range(4):
-        firsts.ready(slot)
-    for item in wd_spread:
+    net.keep(first, first_low)
+    for item in wu_spread:
         item.relay()
     for item in wu_spread + wd_spread:
         item.near()
@@ -576,13 +619,13 @@
         shape((d, 3 * sz.cols), BF16),
         shape((sz.cols, d), BF16),
         shape((d, sz.hid), BF16),
-        shape((sz.hid, d), BF16),
+        shape((sz.hid // 2, d), BF16),
         shape((8, d), F32),
         shape((8, sz.hid), F32),
         shape((r, 3 * sz.cols), BF16),
         shape((r, sz.cols), BF16),
         shape((t, d), F32),
-        shape((r, d), BF16),
+        shape((t, d), BF16),
     )
     scratch = [
         pltpu.VMEM((r, d), BF16),
@@ -597,6 +640,8 @@
         pltpu.VMEM((r, sz.cols), BF16),
         pltpu.VMEM((t, d), F32),
         pltpu.VMEM((t, d), BF16),
+        pltpu.VMEM((sz.row_shard, sz.hid), BF16),
+        pltpu.VMEM((sz.hid_shard // 2, d), BF16),
         *Scatter.scratch(sz),
         pltpu.SemaphoreType.DMA((80 + 28 * sz.nx,)),
         pltpu.SemaphoreType.DMA((80 + 28 * sz.nx,)),
@@ -633,48 +678,81 @@
 
 def feed_forward_kernel(
     sz,
-    first_all, first_in, w_up, w_down, vec_all, bup_all, cot_in,
-    outputs, grad_first_in, grad_low, grad_w_up, grad_w_down, grad_vec,
+    first_low, first_in, w_up, w_down_half, vec_all, bup_all, cot_in, wdown,
+    outputs, grad_first_in, grad_low, grad_w_up, grad_w_down, grad_vec, down_sum, down_in,
     fa, wu, wd, vec, bup, fin, cot, hid, act, gh, g2, g2s, out, gv, dwu, dwd, *rest,
 ):
-    *sum_bufs, send, recv, local = rest
+    *bufs, send, recv, local = rest
+    sum_bufs, bufs = bufs[:7], bufs[7:]
     at = Place(sz)
     net = Copies(send, recv, local)
     t, d, h = sz.tokens, sz.width, sz.half
     two = 2 * t
-    loads = {slot: net.local(first_all.at[pl.ds(slot * two, two), :], fa.at[pl.ds(slot * two, two), :])
-             for slot in (3,)}
+    rf = sz.hid_shard
+    load_first = net.local(first_low, fa.at[pl.ds(0, t), :])
     load_up = net.local(w_up, wu)
     load_bup = net.local(bup_all, bup)
-    for slot in (1, 2, 0):
-        loads[slot] = net.local(
-            first_all.at[pl.ds(slot * two, two), :], fa.at[pl.ds(slot * two, two), :]
-        )
-    load_down = net.local(w_down, wd)
+    load_down = [
+        net.local(w_down_half.at[pl.ds(p * (rf // 2), rf // 2), :], wd.at[pl.ds(p * rf, rf // 2), :])
+        for p in range(sz.parts)
+    ]
+    late_own = pl.ds(at.p * rf + rf // 2, rf // 2)
+    load_down.append(net.local(wdown.at[pl.ds(rf // 2, rf // 2), :], wd.at[late_own, :]))
     load_vec = net.local(vec_all, vec)
     load_fin = net.local(first_in, fin)
     own_rows = pl.ds(at.zh * h, h)
     load_cot = net.local(cot_in.at[at.zh], cot.at[own_rows, :])
-    greet([at.to_c, at.to_y, at.to_z, at.to_h])
-    cot_far = net.remote(cot_in.at[1 - at.zh], cot.at[own_rows, :], at.to_h)
+    greet([at.to_c, at.to_y, at.to_z, at.to_h] + [at.to_x(s) for s in range(1, sz.nx)])
+    load_first.wait()
+    firsts = Gather(net, at, sz, fa, 0, t, tall=True)
+    firsts.send()
+    wd_chunk = rf // 4
+    wd_spread = [
+        Spread(
+            net,
+            at,
+            lambda p, j=j: wd.at[pl.ds(p * rf + j * wd_chunk, wd_chunk), :],
+            wdown.at[pl.ds(j * wd_chunk, wd_chunk), :],
+        )
+        for j in (2, 3)
+    ]
+    for item in wd_spread:
+        item.across()
+        item.along()
     gv[...] = jnp.zeros_like(gv)
 
     sums = Scatter(net, at, sz, sum_bufs)
     load_up.wait()
     load_bup.wait()
-    for slot in (3, 1, 2, 0):
-        loads[slot].wait()
+
+    def project_up(slot):
+        firsts.ready(slot)
         rows = pl.ds(slot * two, two)
 
-        def up(i, rows=rows):
+        def up(i):
             cols = tile(i, 512)
             value = dot(fa[rows, :], wu[:, cols]) + bup[0:1, cols]
             hid[rows, cols] = value
             act[rows, cols] = gate(value).astype(BF16)
 
         loop(sz.hid // 512, up)
-        if slot == 3:
-            load_down.wait()
+
+    project_up(0)
+    firsts.relay()
+    wd_spread[0].relay()
+    project_up(2)
+    project_up(1)
+    firsts.relay_last()
+    project_up(3)
+    wd_spread[1].relay()
+    cot_far = net.remote(cot_in.at[1 - at.zh], cot.at[own_rows, :], at.to_h)
+    for copy in load_down:
+        copy.wait()
+    for item in wd_spread:
+        item.near()
+        item.far()
+    for slot in (3, 1, 2, 0):
+        rows = pl.ds(slot * two, two)
 
         def down(i, rows=rows, slot=slot):
             cols = tile(i, 512)
@@ -750,7 +828,13 @@
 
     loop((sz.hid // 512) * (d // 512), down_grad)
     net.keep(dwd, grad_w_down)
+    down_rows = sz.hid_shard // 4
+    sum_d = Reduce(
+        net, at, lambda p, j: dwd.at[pl.ds(p * sz.hid_shard + j * down_rows, down_rows), :], bufs, 4, True, None
+    )
+    sum_d.start(0)
     sums.send_joined()
+    sum_d.hop(0)
 
     def up_grad(i):
         rows, cols = tile(i // (sz.hid // 512), 512), tile(i % (sz.hid // 512), 512)
@@ -758,6 +842,7 @@
 
     loop((sz.hid // 512) * (d // 512), up_grad)
     net.keep(dwu, grad_w_up)
+    sum_d.hop(1)
     for p in range(sz.parts):
         rf = sz.hid_shard
         gv[8:9, p * sz.slab : p * sz.slab + rf] = jnp.sum(
@@ -782,6 +867,14 @@
     net.keep(g2s, grad_first_in)
     net.keep(out_low, grad_low)
     net.keep(gv, grad_vec)
+    for j in (2, 3):
+        sum_d.add(j)
+    late = pl.ds(2 * down_rows, 2 * down_rows)
+    early = pl.ds(0, 2 * down_rows)
+    net.keep(sum_d.out.at[late, :], down_sum)
+    for j in (0, 1):
+        sum_d.from_h[j].wait_recv()
+    net.keep(sum_d.inn.at[early, :], down_in)
     out_far.wait_recv()
     net.finish()
 
@@ -797,6 +890,8 @@
         shape((d, sz.hid), BF16),
         shape((sz.hid, d), BF16),
         shape((16, d), F32),
+        shape((sz.hid_shard // 2, d), BF16),
+        shape((sz.hid_shard // 2, d), BF16),
     )
     scratch = [
         pltpu.VMEM((r, d), BF16),
@@ -816,14 +911,15 @@
         pltpu.VMEM((d, sz.hid), BF16),
         pltpu.VMEM((sz.hid, d), BF16),
         *Scatter.scratch(sz),
-        pltpu.SemaphoreType.DMA((40,)),
-        pltpu.SemaphoreType.DMA((40,)),
+        *Reduce.scratch(sz, sz.hid_shard, d, BF16, True, 1),
+        pltpu.SemaphoreType.DMA((64 + 8 * sz.nx,)),
+        pltpu.SemaphoreType.DMA((64 + 8 * sz.nx,)),
         pltpu.SemaphoreType.DMA((24,)),
     ]
     return pl.pallas_call(
         functools.partial(feed_forward_kernel, sz),
         out_shape=outs,
-        in_specs=[anywhere] * 7,
+        in_specs=[anywhere] * 8,
         out_specs=[anywhere] * len(outs),
         scratch_shapes=scratch,
         compiler_params=pltpu.CompilerParams(
@@ -841,11 +937,12 @@
         self.result = result
         self.held = held
         self.groups = (at.x * 2 + (1 - at.zh), at.x * 2 + at.zh)
+        self.from_x, self.from_h, self.loads = {}, {}, {}
 
     @staticmethod
-    def scratch(sz, rows, cols, dtype, held):
+    def scratch(sz, rows, cols, dtype, held, kinds=2):
         return [
-            pltpu.VMEM((sz.nx - 1, 2, rows, cols), dtype),
+            pltpu.VMEM((sz.nx - 1, kinds, rows, cols), dtype),
             pltpu.VMEM((2, 8, 128) if held else (2, rows, cols), dtype),
             pltpu.VMEM((rows, cols), dtype),
             pltpu.VMEM((rows, cols), dtype),
@@ -854,24 +951,19 @@
     def chunk(self, j):
         return pl.ds(j * self.rows, self.rows)
 
-    def start(self):
+    def start(self, which):
         at, net = self.at, self.net
-        self.from_x = {}
-        for which in (0, 1):
-            zh = 1 - at.zh if which == 0 else at.zh
-            for j in range(self.chunks):
-                for step in range(1, at.nx):
-                    p = at.x_of(step) * 2 + zh
-                    self.from_x[which, j, step] = net.remote(
-                        self.view(p, j), self.got.at[step - 1, which, self.chunk(j), :], at.to_x(step)
-                    )
-        if not self.held:
-            self.loads = {
-                (which, j): net.local(self.view(self.groups[which], j), self.own.at[which, self.chunk(j), :])
-                for which in (0, 1)
-                for j in range(self.chunks)
-            }
-        self.from_h = {}
+        zh = 1 - at.zh if which == 0 else at.zh
+        for j in range(self.chunks):
+            for step in range(1, at.nx):
+                p = at.x_of(step) * 2 + zh
+                self.from_x[which, j, step] = net.remote(
+                    self.view(p, j), self.got.at[step - 1, which, self.chunk(j), :], at.to_x(step)
+                )
+            if not self.held:
+                self.loads[which, j] = net.local(
+                    self.view(self.groups[which], j), self.own.at[which, self.chunk(j), :]
+                )
 
     def term(self, which, j, i):
         rows = pl.ds(pl.multiple_of(j * self.rows + i * STRIP, STRIP), STRIP)
@@ -889,7 +981,7 @@
         if not self.held:
             self.loads[which, j].wait()
 
-    def hop(self, j):
+    def add(self, j):
         self.ready(0, j)
 
         def body(i):
@@ -897,13 +989,20 @@
             self.out[rows, :] = total.astype(self.out.dtype)
 
         loop(self.rows // STRIP, body)
+
+    def hop(self, j):
+        self.add(j)
+        self.send(j)
+
+    def send(self, j):
         self.from_h[j] = self.net.remote(
             self.out.at[self.chunk(j), :], self.inn.at[self.chunk(j), :], self.at.to_h
         )
 
     def close(self, j):
         self.ready(1, j)
-        self.from_h[j].wait_recv()
+        if j in self.from_h:
+            self.from_h[j].wait_recv()
 
         def body(i):
             rows, total = self.term(1, j, i)
@@ -914,7 +1013,7 @@
 
 def attention_backward_kernel(
     sz,
-    grad_low, grad_first_in, x_all, wqkv, w_out_own, qkv_all, ctx_all, grad_w_up, grad_w_down, grad_vec,
+    grad_low, grad_first_in, x_all, wqkv, w_out_own, qkv_all, ctx_all, grad_w_up, grad_w_down, grad_vec, down_sum, down_in,
     input_grad, out_wqkv, out_wo, out_wup, out_wdown, out_vec, out_bup,
     gb, xs, wq, wo, qkv, ctx, gfi, gv, dctx, dqkv, dk, dv, ig, dwq, dwo, dwo_own, res_q, res_o, res_u, res_d, res_v,
     vec_got, vec_sum, bup_out, *rest,
@@ -934,7 +1033,7 @@
     load_gv = net.local(grad_vec, gv)
     greet([at.peer(f) for f in flips] + [at.to_h] + [at.to_x(s) for s in range(1, sz.nx)])
     load_gb.wait()
-    gather = Gather(net, at, sz, gb, 0, t)
+    gather = Gather(net, at, sz, gb, 0, t, tall=True)
     gather.send()
 
     up_rows, down_rows = sz.slab // 4, rf // 4
@@ -954,13 +1053,19 @@
         net, at, lambda p, j: gv.at[:, pl.ds(pl.multiple_of(p * sz.slab, sz.slab), sz.slab)],
         bufs[16:20], 1, True, res_v,
     )
-    sum_u.start()
-    sum_d.start()
+    late = pl.ds(2 * down_rows, 2 * down_rows)
+    load_sum = net.local(down_sum, sum_d.out.at[late, :])
+    load_in = net.local(down_in, sum_d.inn.at[pl.ds(0, 2 * down_rows), :])
+    sum_u.start(0)
+    load_sum.wait()
+    for j in (2, 3):
+        sum_d.send(j)
+    sum_u.start(1)
     load_x = net.local(x_all, xs)
     load_wq = net.local(wqkv, wq)
     load_gfi = net.local(grad_first_in, gfi)
-    hops = [(s, j) for s in (sum_u, sum_d) for j in range(4)]
-    closes = list(hops)
+    hops = [(sum_u, j) for j in range(4)]
+    closes = [(s, j) for s in (sum_u, sum_d) for j in range(4)]
 
     def pump(count):
         for _ in range(min(count, len(hops))):
@@ -976,11 +1081,13 @@
 
     context_grad(0)
     gather.relay()
+    pump(1)
     context_grad(1)
     context_grad(2)
     gather.relay_last()
     pump(1)
     context_grad(3)
+    pump(1)
     load_qkv.wait()
 
     def attend_back(k):
@@ -1009,13 +1116,13 @@
         dqkv[:, v_cols] = dv[...].astype(BF16)
 
     attend_back(0)
-    pump(1)
+    pump(2)
     for k in range(1, sz.heads):
         attend_back(k)
-    pump(1)
+    pump(2)
     load_wq.wait()
 
-    sums = Scatter(net, at, sz, sum_bufs)
+    sums = Scatter(net, at, sz, sum_bufs, tall=True)
     for slot in (3, 1, 2, 0):
         rows = pl.ds(slot * two, two)
 
@@ -1037,7 +1144,8 @@
         dwq[rows, :] = dot_tn(xs[:, rows], dqkv[...]).astype(BF16)
 
     loop(d // 512, qkv_grad)
-    sum_q.start()
+    sum_q.start(0)
+    sum_d.start(1)
     sums.send_joined()
 
     def out_grad(i):
@@ -1070,9 +1178,14 @@
         gv[1:2, lanes] = jnp.sum(dqkv[:, at_v : at_v + HD].astype(F32), axis=0, keepdims=True)
     for copy in wo_in:
         copy.wait_recv()
-    sum_o.start()
-    sum_v.start()
+    sum_o.start(0)
+    sum_v.start(0)
+    sum_q.hop(0)
+    sum_q.start(1)
+    sum_o.start(1)
+    sum_v.start(1)
     load_gfi.wait()
+    sum_q.hop(1)
     sums.wait()
 
     def final(i):
@@ -1080,14 +1193,14 @@
         ig[rows, :] = (gfi[rows, :] + sums.total(i)).astype(BF16)
 
     loop(t // STRIP, final)
-    pump(8)
     own_rows = pl.ds(at.zh * h, h)
     net.keep(ig.at[own_rows, :], input_grad.at[at.zh])
     ig_far = net.remote(ig.at[pl.ds((1 - at.zh) * h, h), :], input_grad.at[at.zh], at.to_h)
-    for j in range(4):
+    for j in (2, 3):
         sum_q.hop(j)
     sum_o.hop(0)
     sum_v.hop(0)
+    load_in.wait()
 
     for item, j in closes:
         item.close(j)
@@ -1181,7 +1294,7 @@
     return pl.pallas_call(
         functools.partial(attention_backward_kernel, sz),
         out_shape=outs,
-        in_specs=[anywhere] * 10,
+        in_specs=[anywhere] * 12,
         out_specs=[anywhere] * len(outs),
         scratch_shapes=scratch,
         compiler_params=pltpu.CompilerParams(
@@ -1219,14 +1332,14 @@
         )
     vec_pack = jnp.concatenate([low, high], axis=0)
 
-    x_all, wqkv, w_out_own, up_own, down_own, vec_all, bup_all, qkv, ctx, first_in, first_all = attention_forward(
+    x_all, wqkv, w_out_own, up_own, down_own, vec_all, bup_all, qkv, ctx, first_in, first_low = attention_forward(
         sz, inputs, wqkv_pack, wup_pack, w_out, w_down, vec_pack
     )
-    outputs, grad_first_in, grad_low, grad_up, grad_down, grad_vec = feed_forward(
-        sz, first_all, first_in, up_own, down_own, vec_all, bup_all, cotangent
+    outputs, grad_first_in, grad_low, grad_up, grad_down, grad_vec, down_sum, down_in = feed_forward(
+        sz, first_low, first_in, up_own, down_own, vec_all, bup_all, cotangent, w_down
     )
     input_grad, out_wqkv, out_wo, out_wup, out_wdown, out_vec, out_bup = attention_backward(
-        sz, grad_low, grad_first_in, x_all, wqkv, w_out_own, qkv, ctx, grad_up, grad_down, grad_vec
+        sz, grad_low, grad_first_in, x_all, wqkv, w_out_own, qkv, ctx, grad_up, grad_down, grad_vec, down_sum, down_in
     )
 
     def by_rows(which):

time: 546 us -> 478 us (0.88)
  Pallas kernels: 516 us -> 449 us
    pallas_call x1, Pallas kernels: 228 us -> 148 us  [attention_forward(): pl.pallas_call(functools.partial(attention_forward_kernel, sz), out_shape...]
    pallas_call x1, Pallas kernels: 89.7 us -> 137 us  [feed_forward(): pl.pallas_call(functools.partial(feed_forward_kernel, sz), out_shape=outs...]
    pallas_call x1, Pallas kernels: 199 us -> 164 us  [attention_backward(): pl.pallas_call(functools.partial(attention_backward_kernel, sz), out_shap...]
where the time goes in v2:
time: 478 us; the launch traced here: 477 us
  Pallas kernels  449 us (94%)
  local copies, waits for them, and re-layouts  19.7 us (4%)
  other arithmetic  7.84 us (2%)
    pallas_call x1, Pallas kernels, attention_backward(): pl.pallas_call(functools.partial(attention_backward_kernel, sz), out_shap...  164 us
    pallas_call x1, Pallas kernels, attention_forward(): pl.pallas_call(functools.partial(attention_forward_kernel, sz), out_shape...  148 us
    pallas_call x1, Pallas kernels, feed_forward(): pl.pallas_call(functools.partial(feed_forward_kernel, sz), out_shape=outs...  137 us

profile of v2, /device:TPU:17, one launch (start us, length us, event | category | flops | bytes accessed | tf_op | source)
XLA Modules:
  0.0 477.2 jit_solution(14951972867818295448)
XLA Ops:
  0.7 0.0 copy-start.5
  0.7 0.8 stack.46
  1.5 0.7 pad_convert_fusion
  2.2 0.2 dynamic_update_slice.3
  2.4 0.6 pad_maximum_fusion.1.vec_pack
  3.0 1.1 reshape.112
  4.1 0.2 copy.51
  4.3 0.2 reshape.113
  4.5 1.1 reshape.114
  5.6 0.0 copy-start.2
  5.6 0.2 copy.50
  5.8 0.2 reshape.115
  6.0 0.0 copy-done.5
  6.0 0.2 reshape.116
  6.2 0.2 copy.49
  6.4 0.2 reshape.117
  6.6 0.9 pad_maximum_fusion.wqkv_pack
  7.5 0.0 copy-done.2
  7.5 0.3 copy.42
  7.8 0.4 copy.48
  8.2 1.5 reshape.119.wup_pack
  9.7 147.7 %attention_forward.1 = (bf16[1024,2048]{1,0:T(8,128)(2,1)}, bf16[2048,768]{1,0:T(8,128)(2,1)}, bf16[256,2048]{1,0:T(8,128)(2,1)}, bf16[2048,1024]{1,0:T(8,128)(2...) custom-call(bf16[2,64,2048]{2,1,0:T(8,128)(2,1)} %xin.1, ...), custom_call_target="tpu_custom_call" | custom-call | tf_op jit(solution)/shard_map/attention_forward/pallas_call | solution.py:650
  157.5 137.5 %feed_forward.1 = (bf16[2,64,2048]{2,1,0:T(8,128)(2,1)}, f32[128,2048]{1,0:T(8,128)}, bf16[128,2048]{1,0:T(8,128)(2,1)}, bf16[2048,1024]{1,0:T(8,128)(2,1)}, bf1...) custom-call(bf16[128,2048]{1,0:T(8,128)(2,1)} %get-tuple-element.55.first_l, ...), custom_call_target="tpu_custom_call" | custom-call | tf_op jit(solution)/shard_map/feed_forward/pallas_call | solution.py:919
  295.0 163.5 %attention_backward.1 = (bf16[2,64,2048]{2,1,0:T(8,128)(2,1)}, bf16[8,64,768]{2,1,0:T(8,128)(2,1)}, bf16[64,2048]{1,0:T(8,128)(2,1)}, bf16[8,64,1024]{2,1,0:T(8,...) custom-call(bf16[128,2048]{1,0:T(8,128)(2,1)} %get-tuple-element.62.grad_low, ...), custom_call_target="tpu_custom_call" | custom-call | tf_op jit(solution)/shard_map/attention_backward/pallas_call | solution.py:1294
  458.5 0.0 copy-start.3
  458.5 1.3 slice.60
  459.8 0.8 constant_dynamic-slice_fusion
  460.6 0.5 slice_bitcast_fusion
  461.1 2.1 convert_element_type.66
  463.2 1.8 convert_element_type.79
  465.0 0.0 copy-done.3
  465.0 0.2 slice_convert_fusion
  465.2 0.3 reshape.127
  465.5 0.3 copy.40
  465.8 1.0 reshape.123
  466.8 0.3 reshape.126
  467.1 0.3 copy.39
  467.5 0.0 copy-start.1
  467.5 1.0 reshape.122
  468.5 0.3 reshape.125
  468.7 0.3 copy.38
  469.1 1.0 reshape.121
  470.1 0.0 copy-done.1
  470.1 0.9 reshape.128
  471.1 1.2 copy.41
  472.3 0.0 copy-start
  472.3 2.5 copy.43
  474.8 0.0 copy-start.4
  474.8 0.0 copy-done
  474.8 1.6 convert_element_type.84
  476.4 0.0 copy-done.4
  476.4 0.8 copy.54
  (2 shorter events, 0.0 us)
Async XLA Ops:
  0.7 5.3 %copy-start.5 = (bf16[64,2048]{1,0:T(8,128)(2,1)S(1)}, bf16[64,2048]{1,0:T(8,128)(2,1)}, u32[]{:S(2)}) copy-start(bf16[64,2048]{1,0:T(8,128)(2,1)} %param.23) | copy-start | bytes 786436
  5.6 1.9 copy-start.2
  458.5 6.5 %copy-start.3 = (bf16[8,64,768]{2,1,0:T(8,128)(2,1)S(1)}, bf16[8,64,768]{2,1,0:T(8,128)(2,1)}, u32[]{:S(2)}) copy-start(bf16[8,64,768]{2,1,0:T(8,128)(2,1)} %get-tuple-element.75) | copy-start | bytes 2359300
  467.5 2.6 copy-start.1
  472.3 2.5 copy-start
  474.8 1.6 copy-start.4

commit v3 on v2

--- a/solution.py
+++ b/solution.py
@@ -35,6 +35,7 @@
         self.cols = self.heads * HD
         self.hid = hidden // TP
         self.slab = width // self.parts
+        self.by_lanes = self.hid_shard % HD == 0
 
 
 class Place:
@@ -64,6 +65,11 @@
         y = 1 - self.y if flip & 2 else self.y
         c = 1 - self.c if flip & 1 else self.c
         return zl * 4 + y * 2 + c
+
+    def head_lanes(self, sz, member, k):
+        group = member // sz.pieces
+        head = ((member - group * sz.pieces) * sz.heads + k) * (TP // sz.pieces) + group
+        return pl.ds(pl.multiple_of(head * HD, HD), HD)
 
     def to_x(self, step):
         return {"x": lax.rem(self.x + step, self.nx)}
@@ -94,6 +100,33 @@
         copy.start()
         self.sent.append(copy)
         return copy
+
+    def remote_parts(self, pairs, whole, target):
+        i = self.n_remote
+        self.n_remote += 1
+
+        def copy(src, dst):
+            return pltpu.make_async_remote_copy(
+                src_ref=src,
+                dst_ref=dst,
+                send_sem=self.send.at[i],
+                recv_sem=self.recv.at[i],
+                device_id=target,
+                device_id_type=pl.DeviceIdType.MESH,
+            )
+
+        for src, dst in pairs:
+            copy(src, dst).start()
+        total = copy(whole, whole)
+        self.sent.append(total)
+        return total
+
+    def local_parts(self, pairs, whole):
+        i = self.n_local
+        self.n_local += 1
+        for src, dst in pairs:
+            pltpu.make_async_copy(src, dst, self.local_sems.at[i]).start()
+        return pltpu.make_async_copy(whole, whole, self.local_sems.at[i])
 
     def local(self, src, dst):
         i = self.n_local
@@ -370,7 +403,7 @@
 
 def attention_forward_kernel(
     sz,
-    xin, wqkv_pack, wup_pack, wout, wdown, vec_pack,
+    xin, w_query, w_key, w_value, wout, wup_rows, wdown, vec_pack,
     x_all, wqkv, w_out_own, w_up, w_down, vec_all, bup_all, qkv_all, ctx_all, first_in, first_low,
     xs, wq, wo_got, wo, vecs, vec, bup, acc, qkv, ctx, fin, first, wu_own, wd_own, *rest,
 ):
@@ -391,14 +424,35 @@
     def wq_rows(p, member, count=1):
         return pl.ds((p * TP + member) * rw, count * rw)
 
-    own_wq = net.local(wqkv_pack.at[at.t], wq.at[wq_rows(at.p, at.t), :])
+    def wq_parts(member):
+        return [
+            (
+                source.at[:, at.head_lanes(sz, member, k)],
+                wq.at[wq_rows(at.p, at.t), pl.ds(which * sz.cols + k * HD, HD)],
+            )
+            for which, source in enumerate((w_query, w_key, w_value))
+            for k in range(sz.heads)
+        ]
+
+    def wu_parts(member, dst):
+        if not sz.by_lanes:
+            return [(wup_rows.at[member], dst)]
+        return [
+            (
+                wup_rows.at[:, pl.ds(pl.multiple_of((p * TP + member) * rf, rf), rf)],
+                dst.at[:, pl.ds(p * rf, rf)],
+            )
+            for p in range(sz.parts)
+        ]
+
+    wq_mine, wu_mine = wq.at[wq_rows(at.p, at.t), :], w_up.at[wq_rows(at.p, at.t), :]
+    own_wq = net.local_parts(wq_parts(at.t), wq_mine)
     own_vec = net.local(vec_pack, vecs.at[at.p * TP + at.t])
     own_wo = net.local(wout, wo_got.at[at.p])
-    wu_here = net.local(wup_pack.at[at.t], wu_own)
+    wu_here = net.local_parts(wu_parts(at.t, wu_own), wu_own)
     wd_here = net.local(wdown.at[pl.ds(0, rf // 2), :], wd_own)
     wq_in = [None] + [
-        net.remote(wqkv_pack.at[at.index_of(f)], wq.at[wq_rows(at.p, at.t), :], at.peer(f))
-        for f in flips
+        net.remote_parts(wq_parts(at.index_of(f)), wq_mine, at.peer(f)) for f in flips
     ]
     vec_in = [net.remote(vec_pack, vecs.at[at.p * TP + at.t], at.peer(f)) for f in flips]
     own_x.wait()
@@ -442,8 +496,7 @@
     wd_here.wait()
     net.keep(wd_own, w_down.at[pl.ds(at.p * (rf // 2), rf // 2), :])
     wu_in = [None] + [
-        net.remote(wup_pack.at[at.index_of(f)], w_up.at[wq_rows(at.p, at.t), :], at.peer(f))
-        for f in flips
+        net.remote_parts(wu_parts(at.index_of(f), wu_mine), wu_mine, at.peer(f)) for f in flips
     ]
 
     def accumulate(zh, first_part):
@@ -508,10 +561,8 @@
 
     group = at.t // sz.pieces
     member = at.t - group * sz.pieces
-    per = TP // sz.pieces
     for k in range(sz.heads):
-        head = (member * sz.heads + k) * per + group
-        lanes = tile(head, HD)
+        lanes = at.head_lanes(sz, at.t, k)
 
         def biased(i, k=k, lanes=lanes):
             rows = tile(i, 256)
@@ -610,7 +661,7 @@
     net.finish()
 
 
-def attention_forward(sz, xin, wqkv_pack, wup_pack, wout, wdown, vec_pack):
+def attention_forward(sz, *args):
     t, d, r = sz.tokens, sz.width, sz.rows_all
     shape = jax.ShapeDtypeStruct
     anywhere = pl.BlockSpec(memory_space=pl.ANY)
@@ -650,14 +701,14 @@
     return pl.pallas_call(
         functools.partial(attention_forward_kernel, sz),
         out_shape=outs,
-        in_specs=[anywhere] * 6,
+        in_specs=[anywhere] * 8,
         out_specs=[anywhere] * len(outs),
         scratch_shapes=scratch,
         compiler_params=pltpu.CompilerParams(
             collective_id=0, has_side_effects=True, vmem_limit_bytes=VMEM_LIMIT
         ),
         name="attention_forward",
-    )(xin, wqkv_pack, wup_pack, wout, wdown, vec_pack)
+    )(*args)
 
 
 GELU_A = 0.7978845608028654
@@ -1014,7 +1065,7 @@
 def attention_backward_kernel(
     sz,
     grad_low, grad_first_in, x_all, wqkv, w_out_own, qkv_all, ctx_all, grad_w_up, grad_w_down, grad_vec, down_sum, down_in,
-    input_grad, out_wqkv, out_wo, out_wup, out_wdown, out_vec, out_bup,
+    input_grad, out_wq, out_wk, out_wv, out_wo, out_wup, out_wdown, out_vec, out_bup,
     gb, xs, wq, wo, qkv, ctx, gfi, gv, dctx, dqkv, dk, dv, ig, dwq, dwo, dwo_own, res_q, res_o, res_u, res_d, res_v,
     vec_got, vec_sum, bup_out, *rest,
 ):
@@ -1155,7 +1206,6 @@
     loop(d // 512, out_grad)
     group = at.t // sz.pieces
     member = at.t - group * sz.pieces
-    per = TP // sz.pieces
     wo_in = []
     for k in range(sz.heads):
         for f in range(1, sz.pieces):
@@ -1172,7 +1222,7 @@
         ).wait()
     load_gv.wait()
     for k in range(sz.heads):
-        lanes = tile((member * sz.heads + k) * per + group, HD)
+        lanes = at.head_lanes(sz, at.t, k)
         gv[0:1, lanes] = jnp.sum(dqkv[:, k * HD : (k + 1) * HD].astype(F32), axis=0, keepdims=True)
         at_v = 2 * sz.cols + k * HD
         gv[1:2, lanes] = jnp.sum(dqkv[:, at_v : at_v + HD].astype(F32), axis=0, keepdims=True)
@@ -1205,15 +1255,40 @@
     for item, j in closes:
         item.close(j)
     net.keep(res_d, out_wdown)
-    net.keep(res_u.at[pl.ds(at.t * rw, rw), :], out_wup.at[at.t])
+
+    def rows_of(buf, member):
+        return buf.at[pl.ds(member * rw, rw), :]
+
+    def up_parts(member):
+        if not sz.by_lanes:
+            return [(res_u.at[pl.ds(member * rw, rw), :], out_wup.at[at.t])]
+        return [
+            (
+                res_u.at[pl.ds(member * rw, rw), pl.ds(p * rf, rf)],
+                out_wup.at[:, pl.ds(pl.multiple_of((p * TP + at.t) * rf, rf), rf)],
+            )
+            for p in range(sz.parts)
+        ]
+
+    def qkv_parts(member):
+        return [
+            (
+                res_q.at[pl.ds(member * rw, rw), pl.ds(which * sz.cols + k * HD, HD)],
+                target.at[:, at.head_lanes(sz, at.t, k)],
+            )
+            for which, target in enumerate((out_wq, out_wk, out_wv))
+            for k in range(sz.heads)
+        ]
+
+    net.kept.append(net.local_parts(up_parts(at.t), rows_of(res_u, at.t)))
     back_in = [
-        net.remote(res_u.at[pl.ds(at.index_of(f) * rw, rw), :], out_wup.at[at.t], at.peer(f)) for f in flips
+        net.remote_parts(up_parts(at.index_of(f)), rows_of(res_u, at.index_of(f)), at.peer(f)) for f in flips
     ]
     for j in range(4):
         sum_q.close(j)
-    net.keep(res_q.at[pl.ds(at.t * rw, rw), :], out_wqkv.at[at.t])
+    net.kept.append(net.local_parts(qkv_parts(at.t), rows_of(res_q, at.t)))
     back_in += [
-        net.remote(res_q.at[pl.ds(at.index_of(f) * rw, rw), :], out_wqkv.at[at.t], at.peer(f)) for f in flips
+        net.remote_parts(qkv_parts(at.index_of(f)), rows_of(res_q, at.index_of(f)), at.peer(f)) for f in flips
     ]
     sum_o.close(0)
     net.keep(res_o, out_wo)
@@ -1249,9 +1324,11 @@
     anywhere = pl.BlockSpec(memory_space=pl.ANY)
     outs = (
         shape((2, sz.half, d), BF16),
-        shape((TP, rw, wide), BF16),
         shape((rw, d), BF16),
-        shape((TP, rw, sz.hid), BF16),
+        shape((rw, d), BF16),
+        shape((rw, d), BF16),
+        shape((rw, d), BF16),
+        shape((rw, sz.hidden) if sz.by_lanes else (TP, rw, sz.hid), BF16),
         shape((rf, d), BF16),
         shape((8, HD), F32),
         shape((8, rf), F32),
@@ -1304,66 +1381,85 @@
     )(*args)
 
 
+def widen_kernel(count, *refs):
+    for src, dst in zip(refs[:count], refs[count:]):
+        flat = len(src.shape) == 2
+
+        def body(i, src=src, dst=dst, flat=flat):
+            if flat:
+                dst[tile(i, STRIP), :] = src[tile(i, STRIP), :].astype(F32)
+            else:
+                for j in range(src.shape[0]):
+                    dst[j, tile(i, STRIP), :] = src[j, tile(i, STRIP), :].astype(F32)
+
+        loop(src.shape[-2] // STRIP, body)
+
+
+def widen(*arrays):
+    whole = pl.BlockSpec(memory_space=pltpu.VMEM)
+    return pl.pallas_call(
+        functools.partial(widen_kernel, len(arrays)),
+        out_shape=[jax.ShapeDtypeStruct(a.shape, F32) for a in arrays],
+        in_specs=[whole] * len(arrays),
+        out_specs=[whole] * len(arrays),
+        compiler_params=pltpu.CompilerParams(vmem_limit_bytes=VMEM_LIMIT),
+        name="widen",
+    )(*arrays)
+
+
 def per_device(
     sz, inputs, cotangent, w_query, w_key, w_value, w_out, b_query, b_value, b_out, ln1_gain, ln1_bias,
     w_up, b_up, w_down, b_down, ln2_gain, ln2_bias,
 ):
-    rw, rf, d = sz.row_shard, sz.hid_shard, sz.width
-    groups = TP // sz.pieces
+    rw, rf = sz.row_shard, sz.hid_shard
     t = lax.axis_index("zl") * 4 + lax.axis_index("y") * 2 + lax.axis_index("c")
     p = lax.axis_index("x") * 2 + lax.axis_index("zh")
-
-    def by_member(weight):
-        split = weight.reshape(rw, sz.pieces, sz.heads, groups, HD)
-        return split.transpose(3, 1, 0, 2, 4).reshape(TP, rw, sz.cols)
-
-    wqkv_pack = jnp.concatenate([by_member(w) for w in (w_query, w_key, w_value)], axis=2)
-    wup_pack = w_up.reshape(rw, sz.parts, TP, rf).transpose(2, 0, 1, 3).reshape(TP, rw, sz.hid)
-    rows = jnp.stack(
-        [v.astype(F32) for v in (b_query, b_value, b_out, ln1_gain, ln1_bias, b_down, ln2_gain, ln2_bias)]
-    )
-    low = lax.dynamic_update_slice(jnp.zeros((8, HD), F32), rows, (0, (t % sz.pieces) * rw))
+    piece = t % sz.pieces
+    rows = jnp.stack([b_query, b_value, b_out, ln1_gain, ln1_bias, b_down, ln2_gain, ln2_bias]).astype(F32)
+    here = lax.broadcasted_iota(jnp.int32, (8, HD), 1) // rw == piece
+    low = jnp.where(here, jnp.tile(rows, (1, sz.pieces)), 0.0)
     up = b_up.astype(F32)
     if rf >= HD:
-        high = jnp.zeros((8, HD), F32).at[: rf // HD].set(up.reshape(rf // HD, HD))
+        high = jnp.pad(up.reshape(rf // HD, HD), ((0, 8 - rf // HD), (0, 0)))
     else:
-        high = lax.dynamic_update_slice(
-            jnp.zeros((8, HD), F32), up[None], (0, (p % (HD // rf)) * rf)
-        )
+        each = HD // rf
+        here = lax.broadcasted_iota(jnp.int32, (8, HD), 1) // rf == p % each
+        high = jnp.where(here, jnp.tile(up[None], (8, each)), 0.0)
     vec_pack = jnp.concatenate([low, high], axis=0)
 
+    up_rows = w_up
+    if not sz.by_lanes:
+        up_rows = w_up.reshape(rw, sz.parts, TP, rf).transpose(2, 0, 1, 3).reshape(TP, rw, sz.hid)
+
     x_all, wqkv, w_out_own, up_own, down_own, vec_all, bup_all, qkv, ctx, first_in, first_low = attention_forward(
-        sz, inputs, wqkv_pack, wup_pack, w_out, w_down, vec_pack
+        sz, inputs, w_query, w_key, w_value, w_out, up_rows, w_down, vec_pack
     )
     outputs, grad_first_in, grad_low, grad_up, grad_down, grad_vec, down_sum, down_in = feed_forward(
         sz, first_low, first_in, up_own, down_own, vec_all, bup_all, cotangent, w_down
     )
-    input_grad, out_wqkv, out_wo, out_wup, out_wdown, out_vec, out_bup = attention_backward(
-        sz, grad_low, grad_first_in, x_all, wqkv, w_out_own, qkv, ctx, grad_up, grad_down, grad_vec, down_sum, down_in
+    *grads, out_vec, out_bup = attention_backward(
+        sz, grad_low, grad_first_in, x_all, wqkv, w_out_own, qkv, ctx, grad_up, grad_down, grad_vec,
+        down_sum, down_in,
     )
-
-    def by_rows(which):
-        part = out_wqkv[:, :, which * sz.cols : (which + 1) * sz.cols]
-        split = part.reshape(groups, sz.pieces, rw, sz.heads, HD)
-        return split.transpose(2, 1, 3, 0, 4).reshape(rw, d).astype(F32)
-
-    grad_wup = out_wup.reshape(TP, rw, sz.parts, rf).transpose(1, 2, 0, 3).reshape(rw, sz.hidden)
-    vec = lax.dynamic_slice(out_vec, (0, (t % sz.pieces) * rw), (8, rw))
+    input_grad, grad_wq, grad_wk, grad_wv, grad_wo, grad_wup, grad_wdown = widen(*grads)
+    if not sz.by_lanes:
+        grad_wup = grad_wup.reshape(TP, rw, sz.parts, rf).transpose(1, 2, 0, 3).reshape(rw, sz.hidden)
+    vec = lax.dynamic_slice(out_vec, (0, piece * rw), (8, rw))
     return (
         outputs,
-        input_grad.astype(F32),
-        by_rows(0),
-        by_rows(1),
-        by_rows(2),
-        out_wo.astype(F32),
+        input_grad,
+        grad_wq,
+        grad_wk,
+        grad_wv,
+        grad_wo,
         vec[0],
         vec[1],
         vec[2],
         vec[3],
         vec[4],
-        grad_wup.astype(F32),
+        grad_wup,
         out_bup[0],
-        out_wdown.astype(F32),
+        grad_wdown,
         vec[5],
         vec[6],
         vec[7],

time: 478 us -> 461 us (0.964)
  local copies, waits for them, and re-layouts: 19.7 us -> 4.29 us
  other arithmetic: 7.84 us -> 1.28 us
  Pallas kernels: 449 us -> 454 us
    convert_element_type x11 -> x0, local copies, waits for them, and re-layouts: 7.01 us -> none  [the longest x9 4.85 us: by_rows(): return split.transpose(2, 1, 3, 0, 4).reshape(rw, d).astype(F32)]
    pallas_call x0 -> x1, Pallas kernels: none -> 5.65 us  [widen(): pl.pallas_call(functools.partial(widen_kernel, len(arrays)), out_shape=[j...]
    convert_element_type x4 -> x0, other arithmetic: 5.63 us -> none  [the longest x1 2.12 us: per_device(): input_grad.astype(F32)]
    reshape x11 -> x0, local copies, waits for them, and re-layouts: 5.47 us -> none  [the longest x6 3.01 us: by_member(): split = weight.reshape(rw, sz.pieces, sz.heads, groups, HD)]
where the time goes in v3:
time: 461 us; the launch traced here: 460 us
  Pallas kernels  454 us (98%)
    pallas_call x1, Pallas kernels, attention_backward(): pl.pallas_call(functools.partial(attention_backward_kernel, sz), out_shap...  163 us
    pallas_call x1, Pallas kernels, attention_forward(): pl.pallas_call(functools.partial(attention_forward_kernel, sz), out_shape...  148 us
    pallas_call x1, Pallas kernels, feed_forward(): pl.pallas_call(functools.partial(feed_forward_kernel, sz), out_shape=outs...  138 us

profile of v3, /device:TPU:17, one launch (start us, length us, event | category | flops | bytes accessed | tf_op | source)
XLA Modules:
  0.0 460.4 jit_solution(8796672768833692686)
XLA Ops:
  0.7 0.8 stack.35
  1.5 0.7 pad_convert_fusion
  2.2 0.1 tile.10
  2.3 0.6 pad_maximum_fusion.vec_pack
  2.9 147.8 %attention_forward.1 = (bf16[1024,2048]{1,0:T(8,128)(2,1)}, bf16[2048,768]{1,0:T(8,128)(2,1)}, bf16[256,2048]{1,0:T(8,128)(2,1)}, bf16[2048,1024]{1,0:T(8,128)(2...) custom-call(bf16[2,64,2048]{2,1,0:T(8,128)(2,1)} %xin.1, ...), custom_call_target="tpu_custom_call" | custom-call | tf_op jit(solution)/shard_map/attention_forward/pallas_call | solution.py:701
  150.6 137.7 %feed_forward.1 = (bf16[2,64,2048]{2,1,0:T(8,128)(2,1)}, f32[128,2048]{1,0:T(8,128)}, bf16[128,2048]{1,0:T(8,128)(2,1)}, bf16[2048,1024]{1,0:T(8,128)(2,1)}, bf1...) custom-call(bf16[128,2048]{1,0:T(8,128)(2,1)} %get-tuple-element.52.first_l, ...), custom_call_target="tpu_custom_call" | custom-call | tf_op jit(solution)/shard_map/feed_forward/pallas_call | solution.py:970
  288.4 163.0 %attention_backward.1 = (bf16[2,64,2048]{2,1,0:T(8,128)(2,1)}, bf16[64,2048]{1,0:T(8,128)(2,1)}, bf16[64,2048]{1,0:T(8,128)(2,1)}, bf16[64,2048]{1,0:T(8,128)(2,...) custom-call(bf16[128,2048]{1,0:T(8,128)(2,1)} %get-tuple-element.59., ...), custom_call_target="tpu_custom_call" | custom-call | tf_op jit(solution)/shard_map/attention_backward/pallas_call | solution.py:1371
  451.3 0.0 copy-start
  451.4 1.3 slice.32
  452.7 0.7 constant_dynamic-slice_fusion
  453.4 0.5 slice_bitcast_fusion
  454.0 5.7 %widen.1 = (f32[2,64,2048]{2,1,0:T(8,128)}, f32[64,2048]{1,0:T(8,128)}, f32[64,2048]{1,0:T(8,128)}, f32[64,2048]{1,0:T(8,128)}, f32[64,2048]{1,0:T(8,128)}, /*index=5*/f32[64,8192]{1,0:T(8,128)}, f32[256,2048]{1,0:T(8,128)}) custom-call(bf16[2,64,2048]{2,1,0:T(8,128)(2,1)} %get-tuple-element.71.refs_0_, bf16[64,2048]{1,0:T(8,128)(2,1)} %get-tuple-element.72.refs_1_, ...), custom_call_target="tpu_custom_call" | custom-call | tf_op jit(solution)/shard_map/widen/pallas_call | solution.py:1400
  459.6 0.0 copy-done
  459.6 0.8 copy.35
  (4 shorter events, 0.0 us)
Async XLA Ops:
  451.3 8.3 %copy-start = (bf16[2,64,2048]{2,1,0:T(8,128)(2,1)S(1)}, bf16[2,64,2048]{2,1,0:T(8,128)(2,1)}, u32[]{:S(2)}) copy-start(bf16[2,64,2048]{2,1,0:T(8,128)(2,1)} %get-tuple-element.114) | copy-start | bytes 1572868

commit v4 on v3

--- a/solution.py
+++ b/solution.py
@@ -653,8 +653,9 @@
     loop(t // STRIP, norm)
     net.keep(fin, first_in)
     net.keep(first, first_low)
-    for item in wu_spread:
+    for item in wu_spread[:3]:
         item.relay()
+    wu_spread[3].from_h.wait_recv()
     for item in wu_spread + wd_spread:
         item.near()
         item.far()
@@ -741,7 +742,18 @@
     two = 2 * t
     rf = sz.hid_shard
     load_first = net.local(first_low, fa.at[pl.ds(0, t), :])
-    load_up = net.local(w_up, wu)
+
+    def up_rows(p, f):
+        start = (p * TP + at.index_of(f) - at.c) * sz.row_shard
+        return pl.ds(pl.multiple_of(start, 2 * sz.row_shard), 2 * sz.row_shard)
+
+    load_up = []
+    for step in range(sz.nx):
+        for zh in (at.zh, 1 - at.zh):
+            for f in (0, 2, 4, 6):
+                if step == 0 or zh is at.zh or f != 6:
+                    rows = up_rows(at.x_of(step) * 2 + zh, f)
+                    load_up.append(net.local(w_up.at[rows, :], wu.at[rows, :]))
     load_bup = net.local(bup_all, bup)
     load_down = [
         net.local(w_down_half.at[pl.ds(p * (rf // 2), rf // 2), :], wd.at[pl.ds(p * rf, rf // 2), :])
@@ -767,14 +779,21 @@
         )
         for j in (2, 3)
     ]
+    last_up = [
+        net.remote(w_up.at[up_rows(at.pz, 6), :], wu.at[up_rows(at.pz, 6), :], at.to_x(step))
+        for step in range(1, sz.nx)
+    ]
     for item in wd_spread:
         item.across()
         item.along()
     gv[...] = jnp.zeros_like(gv)
 
     sums = Scatter(net, at, sz, sum_bufs)
-    load_up.wait()
     load_bup.wait()
+    for copy in load_up:
+        copy.wait()
+    for copy in last_up:
+        copy.wait_recv()
 
     def project_up(slot):
         firsts.ready(slot)
@@ -843,7 +862,6 @@
     gather = Gather(net, at, sz, g2, 0, t)
     gather.send()
     net.keep(out.at[own_rows, :], outputs.at[at.zh])
-    out_far = net.remote(out.at[pl.ds((1 - at.zh) * h, h), :], outputs.at[at.zh], at.to_h)
     sums.settle()
 
     def back(slot):
@@ -870,6 +888,7 @@
     back(2)
     sums.send_free()
     gather.relay_last()
+    out_far = net.remote(out.at[pl.ds((1 - at.zh) * h, h), :], outputs.at[at.zh], at.to_h)
     back(3)
     sums.send_diag()
 
@@ -963,9 +982,9 @@
         pltpu.VMEM((sz.hid, d), BF16),
         *Scatter.scratch(sz),
         *Reduce.scratch(sz, sz.hid_shard, d, BF16, True, 1),
-        pltpu.SemaphoreType.DMA((64 + 8 * sz.nx,)),
-        pltpu.SemaphoreType.DMA((64 + 8 * sz.nx,)),
-        pltpu.SemaphoreType.DMA((24,)),
+        pltpu.SemaphoreType.DMA((64 + 10 * sz.nx,)),
+        pltpu.SemaphoreType.DMA((64 + 10 * sz.nx,)),
+        pltpu.SemaphoreType.DMA((24 + 12 * sz.nx,)),
     ]
     return pl.pallas_call(
         functools.partial(feed_forward_kernel, sz),
@@ -1116,7 +1135,6 @@
     load_wq = net.local(wqkv, wq)
     load_gfi = net.local(grad_first_in, gfi)
     hops = [(sum_u, j) for j in range(4)]
-    closes = [(s, j) for s in (sum_u, sum_d) for j in range(4)]
 
     def pump(count):
         for _ in range(min(count, len(hops))):
@@ -1245,16 +1263,15 @@
     loop(t // STRIP, final)
     own_rows = pl.ds(at.zh * h, h)
     net.keep(ig.at[own_rows, :], input_grad.at[at.zh])
-    ig_far = net.remote(ig.at[pl.ds((1 - at.zh) * h, h), :], input_grad.at[at.zh], at.to_h)
     for j in (2, 3):
         sum_q.hop(j)
     sum_o.hop(0)
     sum_v.hop(0)
+    ig_far = net.remote(ig.at[pl.ds((1 - at.zh) * h, h), :], input_grad.at[at.zh], at.to_h)
     load_in.wait()
 
-    for item, j in closes:
-        item.close(j)
-    net.keep(res_d, out_wdown)
+    for j in range(4):
+        sum_u.close(j)
 
     def rows_of(buf, member):
         return buf.at[pl.ds(member * rw, rw), :]
@@ -1284,6 +1301,9 @@
     back_in = [
         net.remote_parts(up_parts(at.index_of(f)), rows_of(res_u, at.index_of(f)), at.peer(f)) for f in flips
     ]
+    for j in range(4):
+        sum_d.close(j)
+    net.keep(res_d, out_wdown)
     for j in range(4):
         sum_q.close(j)
     net.kept.append(net.local_parts(qkv_parts(at.t), rows_of(res_q, at.t)))

time: 461 us -> 455 us (0.987)
  Pallas kernels: 454 us -> 448 us
    pallas_call x1, Pallas kernels: 148 us -> 142 us  [attention_forward(): pl.pallas_call(functools.partial(attention_forward_kernel, sz), out_shape...]
where the time goes in v4:
time: 455 us
  Pallas kernels  448 us (98%)
    pallas_call x1, Pallas kernels, attention_backward(): pl.pallas_call(functools.partial(attention_backward_kernel, sz), out_shap...  163 us
    pallas_call x1, Pallas kernels, attention_forward(): pl.pallas_call(functools.partial(attention_forward_kernel, sz), out_shape...  142 us
    pallas_call x1, Pallas kernels, feed_forward(): pl.pallas_call(functools.partial(feed_forward_kernel, sz), out_shape=outs...  137 us

profile of v4, /device:TPU:17, one launch (start us, length us, event | category | flops | bytes accessed | tf_op | source)
XLA Modules:
  0.0 454.8 jit_solution(15335905975281426506)
XLA Ops:
  0.7 0.8 stack.35
  1.5 0.7 pad_convert_fusion
  2.2 0.1 tile.10
  2.3 0.6 pad_maximum_fusion.vec_pack
  2.9 142.1 %attention_forward.1 = (bf16[1024,2048]{1,0:T(8,128)(2,1)}, bf16[2048,768]{1,0:T(8,128)(2,1)}, bf16[256,2048]{1,0:T(8,128)(2,1)}, bf16[2048,1024]{1,0:T(8,128)(2...) custom-call(bf16[2,64,2048]{2,1,0:T(8,128)(2,1)} %xin.1, ...), custom_call_target="tpu_custom_call" | custom-call | tf_op jit(solution)/shard_map/attention_forward/pallas_call | solution.py:702
  145.0 137.3 %feed_forward.1 = (bf16[2,64,2048]{2,1,0:T(8,128)(2,1)}, f32[128,2048]{1,0:T(8,128)}, bf16[128,2048]{1,0:T(8,128)(2,1)}, bf16[2048,1024]{1,0:T(8,128)(2,1)}, bf1...) custom-call(bf16[128,2048]{1,0:T(8,128)(2,1)} %get-tuple-element.52.first_l, ...), custom_call_target="tpu_custom_call" | custom-call | tf_op jit(solution)/shard_map/feed_forward/pallas_call | solution.py:989
  282.3 163.4 %attention_backward.1 = (bf16[2,64,2048]{2,1,0:T(8,128)(2,1)}, bf16[64,2048]{1,0:T(8,128)(2,1)}, bf16[64,2048]{1,0:T(8,128)(2,1)}, bf16[64,2048]{1,0:T(8,128)(2,...) custom-call(bf16[128,2048]{1,0:T(8,128)(2,1)} %get-tuple-element.59., ...), custom_call_target="tpu_custom_call" | custom-call | tf_op jit(solution)/shard_map/attention_backward/pallas_call | solution.py:1391
  445.7 0.0 copy-start
  445.7 1.3 slice.32
  447.0 0.7 constant_dynamic-slice_fusion
  447.8 0.5 slice_bitcast_fusion
  448.3 5.7 %widen.1 = (f32[2,64,2048]{2,1,0:T(8,128)}, f32[64,2048]{1,0:T(8,128)}, f32[64,2048]{1,0:T(8,128)}, f32[64,2048]{1,0:T(8,128)}, f32[64,2048]{1,0:T(8,128)}, /*index=5*/f32[64,8192]{1,0:T(8,128)}, f32[256,2048]{1,0:T(8,128)}) custom-call(bf16[2,64,2048]{2,1,0:T(8,128)(2,1)} %get-tuple-element.71.refs_0_, bf16[64,2048]{1,0:T(8,128)(2,1)} %get-tuple-element.72.refs_1_, ...), custom_call_target="tpu_custom_call" | custom-call | tf_op jit(solution)/shard_map/widen/pallas_call | solution.py:1420
  454.0 0.0 copy-done
  454.0 0.8 copy.35
  (4 shorter events, 0.0 us)
Async XLA Ops:
  445.7 8.3 %copy-start = (bf16[2,64,2048]{2,1,0:T(8,128)(2,1)S(1)}, bf16[2,64,2048]{2,1,0:T(8,128)(2,1)}, u32[]{:S(2)}) copy-start(bf16[2,64,2048]{2,1,0:T(8,128)(2,1)} %get-tuple-element.114) | copy-start | bytes 1572868

commit v5 on v4

--- a/solution.py
+++ b/solution.py
@@ -904,7 +904,6 @@
     )
     sum_d.start(0)
     sums.send_joined()
-    sum_d.hop(0)
 
     def up_grad(i):
         rows, cols = tile(i // (sz.hid // 512), 512), tile(i % (sz.hid // 512), 512)
@@ -912,7 +911,7 @@
 
     loop((sz.hid // 512) * (d // 512), up_grad)
     net.keep(dwu, grad_w_up)
-    sum_d.hop(1)
+    sum_d.hop(0)
     for p in range(sz.parts):
         rf = sz.hid_shard
         gv[8:9, p * sz.slab : p * sz.slab + rf] = jnp.sum(
@@ -937,13 +936,12 @@
     net.keep(g2s, grad_first_in)
     net.keep(out_low, grad_low)
     net.keep(gv, grad_vec)
-    for j in (2, 3):
+    for j in (1, 2, 3):
         sum_d.add(j)
-    late = pl.ds(2 * down_rows, 2 * down_rows)
-    early = pl.ds(0, 2 * down_rows)
+    late = pl.ds(down_rows, 3 * down_rows)
+    early = pl.ds(0, down_rows)
     net.keep(sum_d.out.at[late, :], down_sum)
-    for j in (0, 1):
-        sum_d.from_h[j].wait_recv()
+    sum_d.from_h[0].wait_recv()
     net.keep(sum_d.inn.at[early, :], down_in)
     out_far.wait_recv()
     net.finish()
@@ -960,8 +958,8 @@
         shape((d, sz.hid), BF16),
         shape((sz.hid, d), BF16),
         shape((16, d), F32),
-        shape((sz.hid_shard // 2, d), BF16),
-        shape((sz.hid_shard // 2, d), BF16),
+        shape((sz.hid_shard // 4 * 3, d), BF16),
+        shape((sz.hid_shard // 4, d), BF16),
     )
     scratch = [
         pltpu.VMEM((r, d), BF16),
@@ -1123,12 +1121,12 @@
         net, at, lambda p, j: gv.at[:, pl.ds(pl.multiple_of(p * sz.slab, sz.slab), sz.slab)],
         bufs[16:20], 1, True, res_v,
     )
-    late = pl.ds(2 * down_rows, 2 * down_rows)
+    late = pl.ds(down_rows, 3 * down_rows)
     load_sum = net.local(down_sum, sum_d.out.at[late, :])
-    load_in = net.local(down_in, sum_d.inn.at[pl.ds(0, 2 * down_rows), :])
+    load_in = net.local(down_in, sum_d.inn.at[pl.ds(0, down_rows), :])
     sum_u.start(0)
     load_sum.wait()
-    for j in (2, 3):
+    for j in (1, 2, 3):
         sum_d.send(j)
     sum_u.start(1)
     load_x = net.local(x_all, xs)

time: 455 us -> 445 us (0.978); the launches traced: 455 us -> 439 us
  Pallas kernels: 448 us -> 432 us
    pallas_call x1, Pallas kernels: 163 us -> 151 us  [attention_backward(): pl.pallas_call(functools.partial(attention_backward_kernel, sz), out_shap...]
where the time goes in v5:
time: 445 us; the launch traced here: 439 us
  Pallas kernels  432 us (97%)
    pallas_call x1, Pallas kernels, attention_backward(): pl.pallas_call(functools.partial(attention_backward_kernel, sz), out_shap...  151 us
    pallas_call x1, Pallas kernels, attention_forward(): pl.pallas_call(functools.partial(attention_forward_kernel, sz), out_shape...  142 us
    pallas_call x1, Pallas kernels, feed_forward(): pl.pallas_call(functools.partial(feed_forward_kernel, sz), out_shape=outs...  134 us

profile of v5, /device:TPU:17, one launch (start us, length us, event | category | flops | bytes accessed | tf_op | source)
XLA Modules:
  0.0 438.8 jit_solution(187370466658668379)
XLA Ops:
  0.7 0.8 stack.35
  1.5 0.7 pad_convert_fusion
  2.2 0.1 tile.10
  2.3 0.6 pad_maximum_fusion.vec_pack
  2.9 142.1 %attention_forward.1 = (bf16[1024,2048]{1,0:T(8,128)(2,1)}, bf16[2048,768]{1,0:T(8,128)(2,1)}, bf16[256,2048]{1,0:T(8,128)(2,1)}, bf16[2048,1024]{1,0:T(8,128)(2...) custom-call(bf16[2,64,2048]{2,1,0:T(8,128)(2,1)} %xin.1, ...), custom_call_target="tpu_custom_call" | custom-call | tf_op jit(solution)/shard_map/attention_forward/pallas_call | solution.py:702
  145.0 133.9 %feed_forward.1 = (bf16[2,64,2048]{2,1,0:T(8,128)(2,1)}, f32[128,2048]{1,0:T(8,128)}, bf16[128,2048]{1,0:T(8,128)(2,1)}, bf16[2048,1024]{1,0:T(8,128)(2,1)}, bf1...) custom-call(bf16[128,2048]{1,0:T(8,128)(2,1)} %get-tuple-element.52.first_lo, ...), custom_call_target="tpu_custom_call" | custom-call | tf_op jit(solution)/shard_map/feed_forward/pallas_call | solution.py:987
  278.9 150.8 %attention_backward.1 = (bf16[2,64,2048]{2,1,0:T(8,128)(2,1)}, bf16[64,2048]{1,0:T(8,128)(2,1)}, bf16[64,2048]{1,0:T(8,128)(2,1)}, bf16[64,2048]{1,0:T(8,128)(2,...) custom-call(bf16[128,2048]{1,0:T(8,128)(2,1)} %get-tuple-element.59., ...), custom_call_target="tpu_custom_call" | custom-call | tf_op jit(solution)/shard_map/attention_backward/pallas_call | solution.py:1389
  429.7 0.0 copy-start
  429.7 1.3 slice.32
  431.0 0.8 constant_dynamic-slice_fusion
  431.8 0.5 slice_bitcast_fusion
  432.3 5.7 %widen.1 = (f32[2,64,2048]{2,1,0:T(8,128)}, f32[64,2048]{1,0:T(8,128)}, f32[64,2048]{1,0:T(8,128)}, f32[64,2048]{1,0:T(8,128)}, f32[64,2048]{1,0:T(8,128)}, /*index=5*/f32[64,8192]{1,0:T(8,128)}, f32[256,2048]{1,0:T(8,128)}) custom-call(bf16[2,64,2048]{2,1,0:T(8,128)(2,1)} %get-tuple-element.71.refs_0_, bf16[64,2048]{1,0:T(8,128)(2,1)} %get-tuple-element.72.refs_1_, ...), custom_call_target="tpu_custom_call" | custom-call | tf_op jit(solution)/shard_map/widen/pallas_call | solution.py:1418
  438.0 0.0 copy-done
  438.0 0.8 copy.35
  (4 shorter events, 0.0 us)
Async XLA Ops:
  429.7 8.3 %copy-start = (bf16[2,64,2048]{2,1,0:T(8,128)(2,1)S(1)}, bf16[2,64,2048]{2,1,0:T(8,128)(2,1)}, u32[]{:S(2)}) copy-start(bf16[2,64,2048]{2,1,0:T(8,128)(2,1)} %get-tuple-element.114) | copy-start | bytes 1572868
